TPU v7x, 512 devices: a whole 4x8x8 slice. The times are simulated.
512 devices in a mesh: lat: 16 (over x, y_hi, core), lon: 32 (over z, y_lo).
Axes of the slice: x: 4, y: 8 (y_hi: 2, y_lo: 4; y = y_hi * 4 + y_lo), z: 8, core: 2. Of those that a mesh axis runs over, the one named last changes fastest.
Arguments:
- fields: bfloat16 [368, 1024, 256], P('lat', 'lon'), may hold values from -6 to 6
- conv_weight: bfloat16 [3, 3, 256, 256], replicated, may hold values from -0.21875 to 0.21875
- spectral_gain: float32 [512, 256], replicated, may hold values from 0.25 to 4
- support: int32 [368], P('lat'), may hold values from 1 to 24, as said below
Outputs:
- mixed: bfloat16 [368, 1024, 256], P('lat', 'lon')
Inputs may be any that keep to these rules, and one draw needn't show every extreme that they name: support[i] is the longitude half-width, in cells, of cycle i's convolution support.
All inputs are finite; a program needn't handle non-finite values.
Results may differ from a plain program's by a relative error of at most 0.015.
Values may be sent and summed in bfloat16 or wider, within the bound.
A program may use at most 128 MiB of HBM per device.

v0:
```python
import math

import jax
import jax.numpy as jnp
from jax import lax
from jax.sharding import PartitionSpec as P

NLAT = 368
NLON = 1024
M = 512
SMAX = 24


def extended_2(block, sides, width, periodic):
    for axis, dim in sides:
        count = lax.axis_size(axis)
        forward = [(i, i + 1) for i in range(count - 1)]
        if periodic:
            forward.append((count - 1, 0))
        backward = [(target, source) for source, target in forward]
        low = lax.ppermute(
            lax.slice_in_dim(block, block.shape[dim] - width, None, axis=dim), axis, forward
        )
        high = lax.ppermute(lax.slice_in_dim(block, 0, width, axis=dim), axis, backward)
        block = jnp.concatenate([low, block, high], axis=dim)
    return block


def band_weights(offset, half_width):
    span_len = (half_width + 1).astype(jnp.float32)
    distance = jnp.abs(offset).astype(jnp.float32)
    inside = jnp.abs(offset) <= half_width
    triangle = jnp.where(inside, (span_len - distance) / span_len, 0.0)
    odd_basis = offset.astype(jnp.float32) * triangle / span_len
    box_basis = jnp.where(inside, 1.0, 0.0) / jnp.sqrt(2.0 * half_width.astype(jnp.float32) + 1.0)
    return jnp.stack([triangle, odd_basis, box_basis], axis=0).astype(jnp.bfloat16)


def legendre_table(orders, cosines, cycle_sines, degrees):
    order_real = orders.astype(jnp.float32)[:, None]
    log_start = (
        0.5 * jnp.log((2.0 * order_real + 1.0) / 2.0)
        + 0.5
        * (
            lax.lgamma(2.0 * order_real + 1.0)
            - 2.0 * order_real * math.log(2.0)
            - 2.0 * lax.lgamma(order_real + 1.0)
        )
        + order_real * jnp.log(cycle_sines)[None, :]
    )
    start_scale = jnp.minimum(log_start, 0.0)
    diagonal_start = jnp.exp(log_start - start_scale)
    shrink = 2.0 ** (-24)
    shrink_log = 24.0 * math.log(2.0)

    def recurrence(previous, degree):
        latest, before, log_scale = previous
        degree_real = degree.astype(jnp.float32)
        lower_gap = (degree - orders)[:, None]
        upper_sum = (degree + orders)[:, None]
        divisor = jnp.maximum((lower_gap * upper_sum).astype(jnp.float32), 1.0)
        rise_factor = jnp.sqrt((2.0 * degree_real + 1.0) * (2.0 * degree_real - 1.0) / divisor)
        fall_factor = jnp.sqrt(
            jnp.maximum(
                (2.0 * degree_real + 1.0) * ((lower_gap - 1) * (upper_sum - 1)).astype(jnp.float32),
                0.0,
            )
            / (jnp.maximum(2.0 * degree_real - 3.0, 1.0) * divisor)
        )
        current = rise_factor * cosines[None, :] * latest - fall_factor * before
        current = jnp.where(lower_gap == 0, diagonal_start, current)
        current = jnp.where(lower_gap < 0, 0.0, current)
        log_scale = jnp.where(lower_gap == 0, start_scale, log_scale)
        value = current * jnp.exp(log_scale)
        too_big = jnp.abs(current) > 2.0**24
        next_latest = jnp.where(too_big, current * shrink, current)
        next_before = jnp.where(too_big, latest * shrink, latest)
        next_scale = jnp.where(too_big, log_scale + shrink_log, log_scale)
        return ((next_latest, next_before, next_scale), value)

    blank = jnp.zeros_like(diagonal_start)
    _, stacked_rows = lax.scan(
        recurrence, (blank, blank, blank), jnp.arange(degrees, dtype=jnp.int32), unroll=32
    )
    return jnp.transpose(stacked_rows, (1, 0, 2))


def split_pair(table):
    upper_part = table.astype(jnp.bfloat16)
    lower_part = (table - upper_part.astype(jnp.float32)).astype(jnp.bfloat16)
    return (upper_part, lower_part)


def paired_einsum(form, data, table_pair):
    first = jnp.einsum(form, data, table_pair[0], preferred_element_type=jnp.float32)
    second = jnp.einsum(form, data, table_pair[1], preferred_element_type=jnp.float32)
    return first + second


def legendre_apply(
    spread, first_order, order_count, local_gain, cycle_weight, cosines, cycle_sines
):
    orders = first_order + jnp.arange(order_count, dtype=jnp.int32)
    legendre = legendre_table(orders, cosines, cycle_sines, M)
    weighted_pair = split_pair(legendre * cycle_weight[None, None, :])
    plain_pair = split_pair(legendre)
    channel_count, cycle_total, _ = spread.shape
    values = spread.reshape(channel_count, cycle_total, order_count, 2)
    forward = paired_einsum("cxmp,mlx->mplc", values, weighted_pair)
    filtered = (forward * local_gain[None, None, :, :]).astype(jnp.bfloat16)
    returned = paired_einsum("mplc,mlx->cxmp", filtered, plain_pair)
    return returned.astype(jnp.bfloat16).reshape(channel_count, cycle_total, 2 * order_count)


def per_device(fields, conv_weight, spectral_gain, support):
    lat_rows, lon_cols, channels = fields.shape
    lat_index = lax.axis_index("lat")
    lon_index = lax.axis_index("lon")
    lat_count = lax.axis_size("lat")
    lon_count = lax.axis_size("lon")
    full_cycles = lax.all_to_all(fields, "lon", split_axis=2, concat_axis=1, tiled=True)
    lon_position = jnp.arange(NLON, dtype=jnp.int32)
    order_position = jnp.arange(M, dtype=jnp.int32)
    phase_index = lon_position[:, None] * order_position[None, :] % NLON
    phase_angle = phase_index.astype(jnp.float32) * (2.0 * math.pi / NLON)
    forward_table = (
        jnp.stack([jnp.cos(phase_angle), jnp.sin(phase_angle)], axis=2).reshape(NLON, 2 * M) / NLON
    )
    fourier_rows = paired_einsum("yjc,jk->cyk", full_cycles, split_pair(forward_table)).astype(
        jnp.bfloat16
    )
    colatitude = (jnp.arange(NLAT, dtype=jnp.float32) + 0.5) * (math.pi / NLAT)
    cosines = jnp.cos(colatitude)
    cycle_sines = jnp.sin(colatitude)
    cycle_weight = cycle_sines * (math.pi / NLAT)
    spread = lax.all_to_all(
        lax.all_to_all(fourier_rows, "lon", split_axis=2, concat_axis=0, tiled=True),
        "lat",
        split_axis=0,
        concat_axis=1,
        tiled=True,
    )
    order_count = M // lon_count
    channel_block = channels // lat_count
    local_gain = lax.dynamic_slice_in_dim(
        spectral_gain, lat_index * channel_block, channel_block, 1
    )
    synthesis = legendre_apply(
        spread, lon_index * order_count, order_count, local_gain, cycle_weight, cosines, cycle_sines
    )
    gathered = lax.all_to_all(
        lax.all_to_all(synthesis, "lat", split_axis=1, concat_axis=0, tiled=True),
        "lon",
        split_axis=0,
        concat_axis=2,
        tiled=True,
    )
    order_weight = jnp.where(order_position == 0, 1.0, 2.0)
    inverse_table = (
        jnp.stack([jnp.cos(phase_angle.T), jnp.sin(phase_angle.T)], axis=1)
        * order_weight[:, None, None]
    ).reshape(2 * M, NLON)
    spectral_cols = paired_einsum("cyk,kj->yjc", gathered, split_pair(inverse_table)).astype(
        jnp.bfloat16
    )
    wide_rows = extended_2(fields, (("lon", 1),), SMAX, True)
    extended = extended_2(wide_rows, (("lat", 0),), 1, False)
    target = lax.broadcasted_iota(jnp.int32, (lon_cols, lon_cols + 2 * SMAX), 0)
    source = lax.broadcasted_iota(jnp.int32, (lon_cols, lon_cols + 2 * SMAX), 1)
    offset = source - target - SMAX
    band_table = band_weights(offset[None], support[:, None, None])
    stacked = jnp.stack([extended[lat_step : lat_step + lat_rows] for lat_step in range(3)], 0)
    pooled = jnp.einsum(
        "kyje,ayec->yjakc", band_table, stacked, preferred_element_type=jnp.float32
    ).astype(jnp.bfloat16)
    convolved = jnp.dot(
        pooled.reshape(lat_rows * lon_cols, 9 * channels),
        conv_weight.reshape(9 * channels, channels),
        preferred_element_type=jnp.float32,
    )
    spectral = lax.all_to_all(spectral_cols, "lon", split_axis=1, concat_axis=2, tiled=True)
    total = convolved.reshape(lat_rows, lon_cols, channels) + spectral.astype(jnp.float32)
    return (fields.astype(jnp.float32) + jax.nn.gelu(total, approximate=False)).astype(jnp.bfloat16)


def solution(mesh):
    placed = (P("lat", "lon", None), P(), P(), P("lat"))
    return jax.shard_map(
        per_device, mesh=mesh, in_specs=placed, out_specs=P("lat", "lon", None), check_vma=False
    )
```

profile of v0, /device:TPU:1, one launch (start us, length us, event | category | flops | bytes accessed | tf_op | source)
XLA Modules:
  0.0 1710.9 jit_solution(11277706629877935252)
XLA Ops:
  3.8 14.3 all-to-all-start
  18.1 8.2 fusion.327
  26.3 2.8 fusion.276
  29.0 6.3 copy.101
  35.3 4.1 convert_element_type.1417
  39.4 6.3 copy.95
  45.7 4.3 convert_element_type.1414
  53.7 2.9 reshape.2127
  56.6 2.6 fusion.290
  60.1 2.5 copy.104
  62.6 5.1 reshape.2134
  67.7 9.8 all-to-all-start.1
  77.7 12.0 all-to-all-done.1
  89.7 6.2 reshape.2135
  95.9 3.8 copy.106
  101.9 3.6 reshape.2136
  105.5 10.7 all-to-all-start.2
  116.3 1412.6 %while.23 = (s32[]{:T(128)}, f32[16,368]{1,0:T(8,128)S(1)}, f32[16,368]{1,0:T(8,128)S(1)}, f32[16,368]{1,0:T(8,128)S(1)}, f32[16,32,16,368]{3,2,1,0:T(8,128)}, /...) while((s32[]{:T(128)}, f32[16,368]{1,0:T(8,128)S(1)}, ...), condition=%wide.region_1.2_spmd.clone.clone.clone.clone, body=%wide.region_0.1_spmd.clone.clone.clone.clone.sunk | while | flops 4882626 | bytes 6250758 | solution.py:82
  1528.9 12.6 copy.94
  1541.8 3.0 reshape.2137
  1544.9 5.3 copy.109
  1550.2 3.6 reshape.2107
  1553.8 5.8 fusion.269
  1559.6 5.8 fusion.306
  1572.2 9.6 all-to-all-start.3
  1582.7 2.9 collective-permute-start
  1585.6 6.5 collective-permute-start.1
  1592.2 8.2 fusion.329
  1600.3 2.5 subtract_convert_fusion.1
  1605.1 2.4 reshape.2140
  1607.5 3.9 all-to-all-start.4
  1611.9 5.1 copy.93
  1617.0 4.1 reshape.2123
  1621.1 5.1 copy.118
  1626.1 4.1 reshape.2124
  1637.7 2.9 reshape.2128
  1643.5 2.5 copy.120
  1646.1 5.3 reshape.2142
  1651.4 9.5 all-to-all-start.5
  1663.4 8.5 collective-permute-start.2
  1674.2 7.0 collective-permute-done.3
  1681.2 2.6 fusion.332
  1683.8 6.2 reshape.2143
  1690.0 3.0 copy.121
  1693.0 2.6 reshape.2110
  1695.6 6.1 copy.146
  1701.7 3.1 copy.123
  1704.8 5.9 fusion.336
  (1712 shorter events, 1109.9 us)
Async XLA Ops:
  0.0 1704.8 %copy-start = (bf16[3,3,256,256]{3,2,1,0:T(8,128)(2,1)S(1)}, bf16[3,3,256,256]{3,2,1,0:T(8,128)(2,1)}, u32[]{:S(2)}) copy-start(bf16[3,3,256,256]{3,2,1,0:T(8,128)(2,1)} %param.7) | copy-start | bytes 3538948
  3.8 46.2 %all-to-all-start = ((bf16[32,2,2944]{2,1,0:T(2,128)(2,1)}), bf16[32,2,2944]{2,1,0:T(2,128)(2,1)S(1)}, u32[]{:S(2)}, u32[]{:S(2)}) async-start(bf16[32,2,2944]{2,1,0:T(2,128)(2,1)} %reshape.2132), calls=%async_computation | async-start | bytes 753664 | tf_op jit(solution)/shard_map/all_to_all | solution.py:121
  56.6 2.6 copy-start.4
  67.7 22.0 %all-to-all-start.1 = ((bf16[32,2,2944]{2,1,0:T(2,128)(2,1)}), bf16[32,2,2944]{2,1,0:T(2,128)(2,1)S(1)}, u32[]{:S(2)}, u32[]{:S(2)}) async-start(bf16[32,2,2944]{2,1,0:T(2,128)(2,1)} %reshape.2134), calls=%async_computation.1 | async-start | bytes 753664 | tf_op jit(solution)/shard_map/all_to_all | solution.py:137
  101.9 14.4 copy-start.2
  101.9 14.4 copy-start.5
  105.5 1436.3 %all-to-all-start.2 = ((bf16[16,2,5888]{2,1,0:T(2,128)(2,1)}), bf16[16,2,5888]{2,1,0:T(2,128)(2,1)}, u32[]{:S(2)}, u32[]{:S(2)}) async-start(bf16[16,2,5888]{2,1,0:T(2,128)(2,1)} %reshape.2136), calls=%async_computation.2 | async-start | bytes 753664 | tf_op jit(solution)/shard_map/all_to_all | solution.py:136
  1528.9 12.7 copy-start.6
  1553.7 11.7 slice-start
  1553.8 11.7 slice-start.1
  1559.6 5.8 slice-start.2
  1569.2 12.7 copy-start.1
  1572.2 30.6 %all-to-all-start.3 = ((bf16[16,2,5888]{2,1,0:T(2,128)(2,1)}), bf16[16,2,5888]{2,1,0:T(2,128)(2,1)S(1)}, u32[]{:S(2)}, u32[]{:S(2)}) async-start(bf16[16,2,5888]{2,1,0:T(2,128)(2,1)} %reshape.2138), calls=%async_computation.3 | async-start | bytes 753664 | tf_op jit(solution)/shard_map/all_to_all | solution.py:152
  1582.7 48.8 %collective-permute-start = (bf16[23,24,256]{2,1,0:T(8,128)(2,1)}, bf16[23,24,256]{2,1,0:T(8,128)(2,1)}, u32[]{:S(2)}, u32[]{:S(2)}) collective-permute-start(bf16[23,24,256]{2,1,0:T(8,128)(2,1)} %get-tuple-element.825), channel_id=1, source_target_pairs={{0,1},{1,2},{2,3},{3,4},{4,5},{5,6},{6,7},{7,8},{8,9},{9,10},{10,1... | collective-permute-start | bytes 847880 | tf_op jit(solution)/shard_map/ppermute | solution.py:21
  1585.6 75.3 %collective-permute-start.1 = (bf16[23,24,256]{2,1,0:T(8,128)(2,1)}, bf16[23,24,256]{2,1,0:T(8,128)(2,1)}, u32[]{:S(2)}, u32[]{:S(2)}) collective-permute-start(bf16[23,24,256]{2,1,0:T(8,128)(2,1)} %get-tuple-element.824), channel_id=1, source_target_pairs={{1,0},{2,1},{3,2},{4,3},{5,4},{6,5},{7,6},{8,7},{9,8},{10,9},{11,1... | collective-permute-start | bytes 847880 | tf_op jit(solution)/shard_map/ppermute | solution.py:24
  1605.1 6.3 copy-start.8
  1607.5 26.6 %all-to-all-start.4 = ((bf16[32,2,2944]{2,1,0:T(2,128)(2,1)}), bf16[32,2,2944]{2,1,0:T(2,128)(2,1)S(1)}, u32[]{:S(2)}, u32[]{:S(2)}) async-start(bf16[32,2,2944]{2,1,0:T(2,128)(2,1)} %reshape.2140), calls=%async_computation.4 | async-start | bytes 753664 | tf_op jit(solution)/shard_map/all_to_all | solution.py:151
  1640.6 2.3 copy-start.3
  1646.0 27.8 %copy-start.7 = (f32[32,80]{1,0:T(8,128)S(1)}, f32[32,80]{1,0:T(8,128)}, u32[]{:S(2)}) copy-start(f32[32,80]{1,0:T(8,128)} %fusion.361) | copy-start | bytes 30724
  1646.0 27.8 %copy-start.9 = (s32[23]{0:T(128)S(1)}, s32[23]{0:T(128)}, u32[]{:S(2)}) copy-start(s32[23]{0:T(128)} %param.9) | copy-start | bytes 280
  1646.1 27.9 %copy-start.10 = (f32[23]{0:T(128)S(1)}, f32[23]{0:T(128)}, u32[]{:S(2)}) copy-start(f32[23]{0:T(128)} %add_convert_fusion.2) | copy-start | bytes 280
  1646.1 27.9 %copy-start.11 = (f32[23]{0:T(128)S(1)}, f32[23]{0:T(128)}, u32[]{:S(2)}) copy-start(f32[23]{0:T(128)} %add_sqrt_fusion) | copy-start | bytes 280
  1651.4 32.4 %all-to-all-start.5 = ((bf16[32,2,2944]{2,1,0:T(2,128)(2,1)}), bf16[32,2,2944]{2,1,0:T(2,128)(2,1)S(1)}, u32[]{:S(2)}, u32[]{:S(2)}) async-start(bf16[32,2,2944]{2,1,0:T(2,128)(2,1)} %reshape.2142), calls=%async_computation.5 | async-start | bytes 753664 | tf_op jit(solution)/shard_map/all_to_all | solution.py:181
  1663.4 10.7 collective-permute-start.2
  1672.0 9.2 collective-permute-start.3
where the time goes:
time: 1740 us; the launch traced here: 1710 us
  other arithmetic  1060 us (61%)
  loops' own time  339 us (19%)
  local copies, waits for them, and re-layouts  185 us (11%)
  starting transfers between devices  77.7 us (4%)
  matrix products  27.5 us (2%)
  waiting for transfers between devices  19.1 us (1%)
    another operation x1, loops' own time, legendre_table(): lax.scan(recurrence, (blank, blank, blank), jnp.arange(degrees, dtype=jnp...  339 us
    eq x512, other arithmetic, recurrence(): current = jnp.where(lower_gap == 0, diagonal_start, current)  329 us
    sqrt x256, other arithmetic, recurrence(): jnp.sqrt(jnp.maximum((2.0 * degree_real + 1.0) * ((lower_gap - 1) * (uppe...  328 us
    sqrt x256, other arithmetic, recurrence(): jnp.sqrt((2.0 * degree_real + 1.0) * (2.0 * degree_real - 1.0) / divisor)  328 us
    while x496, other arithmetic  47 us
    unnamed x45, local copies, waits for them, and re-layouts  43.9 us
  transfers between devices with their start and end apart: 10, of which 2 were waited for; matrix products, arithmetic and copies ran while one was open for 69% of the time, Pallas kernels for 0%

commit v1 on v0

v1 whole, which is shorter than its diff:
```python
import functools
import math

import jax
import jax.numpy as jnp
import numpy as np
from jax import lax
from jax.experimental import pallas as pl
from jax.experimental.pallas import tpu as pltpu
from jax.sharding import PartitionSpec as P

NLAT = 368
NLON = 1024
M = 512
SMAX = 24
LAT = 16
LON = 32
ROWS = 23
PAD = 24
COLS = 32
HALF = 128
X = LAT * PAD
MESH = pl.DeviceIdType.MESH


def split_pair(table):
    upper_part = table.astype(jnp.bfloat16)
    lower_part = (table - upper_part.astype(jnp.float32)).astype(jnp.bfloat16)
    return upper_part, lower_part


def doubled(table):
    upper = table.astype(jnp.bfloat16)
    lower = (table - upper.astype(np.float32)).astype(jnp.bfloat16)
    return np.concatenate([upper, lower], axis=-1)


def orders_of(bin_index, lat_index):
    first = bin_index + 32 * lat_index
    second = (496 if bin_index == 0 else 512) - first
    return first, second


@functools.lru_cache
def longitude_tables():
    turn = 2.0 * np.pi / NLON
    b = np.arange(32)
    step_one = np.zeros((2, 16, 32))
    for q in range(16):
        step_one[0, q] = np.cos(2 * np.pi * b * q / 32)
        step_one[1, q] = np.sin(2 * np.pi * b * q / 32) if q else (-1.0) ** b
    step_one = step_one.reshape(32, 32)
    r = np.arange(32)
    step_two = np.zeros((16, 2, 2, 16, 2, 32))
    weight = np.zeros((16, 2, 2, 16))
    for q in range(16):
        for a in range(16):
            for u, m in enumerate(orders_of(q, a)):
                cos, sin = np.cos(turn * ((m * r) % NLON)), np.sin(turn * ((m * r) % NLON))
                weight[q, u, :, a] = 1.0 if m == 0 else 2.0
                if q == 0:
                    step_two[q, u, 0, a, u] = cos
                    step_two[q, u, 1, a, u] = sin
                else:
                    sign = 1.0 if u == 0 else -1.0
                    step_two[q, u, 0, a, 0] = cos
                    step_two[q, u, 0, a, 1] = -sign * sin
                    step_two[q, u, 1, a, 0] = sin
                    step_two[q, u, 1, a, 1] = sign * cos
    step_two = step_two.reshape(16, 64, 64)
    back = np.swapaxes(step_two * weight.reshape(16, 64, 1), 1, 2)
    f32 = np.float32
    return (
        doubled(step_one.astype(f32)),
        doubled((step_two / NLON).astype(f32)),
        doubled(back.astype(f32)),
        doubled(step_one.T.astype(f32)),
    )


@functools.lru_cache
def cycle_tables():
    t = np.pi * (np.arange(NLAT) + 0.5) / NLAT
    cos = np.zeros((LAT, PAD))
    log_sin = np.full((LAT, PAD), 0.0)
    weight = np.zeros((LAT, PAD))
    cos[:, :ROWS] = np.cos(t).reshape(LAT, ROWS)
    log_sin[:, :ROWS] = np.log(np.sin(t)).reshape(LAT, ROWS)
    weight[:, :ROWS] = (np.sin(t) * np.pi / NLAT).reshape(LAT, ROWS)
    valid = np.zeros((LAT, PAD))
    valid[:, :ROWS] = 1.0
    k = np.arange(1, M)
    log_norm = np.concatenate([[0.0], np.cumsum(np.log((2 * k - 1) / (2 * k)))])
    log_norm = 0.5 * np.log((2 * np.arange(M) + 1) / 2) + 0.5 * log_norm
    f32 = np.float32
    return (
        cos.reshape(1, X).astype(f32),
        log_sin.reshape(1, X).astype(f32),
        weight.astype(f32),
        valid.reshape(1, X).astype(f32),
        log_norm.astype(f32),
    )


def legendre_kernel(orders, rise, fall, cos_ref, start_ref, scale_ref, upper, lower, table):
    first = lax.broadcasted_iota(jnp.int32, (2, X), 0) == 0
    cosines = cos_ref[...]
    diagonal = start_ref[...]
    start_scale = scale_ref[...]
    order = [orders[0], orders[1]]

    def pair(one, two):
        return jnp.where(first, one, two)

    def steps(block, state):
        latest, before, log_scale = state
        factor = jnp.exp(log_scale)
        for k in range(4):
            degree = block * 4 + k
            up = pair(rise[0, degree], rise[1, degree]) * cosines
            down = pair(fall[0, degree], fall[1, degree])
            on = pair(
                jnp.where(order[0] == degree, 1.0, 0.0), jnp.where(order[1] == degree, 1.0, 0.0)
            )
            current = up * latest + (on * diagonal - down * before)
            value = current * factor
            for lane in range(X // HALF):
                table[lane, pl.ds(2 * degree, 2), :] = value[:, lane * HALF : (lane + 1) * HALF]
            latest, before = current, latest
        too_big = jnp.abs(latest) > 2.0**24
        shrink = jnp.where(too_big, 2.0**-24, 1.0)
        log_scale = jnp.where(too_big, log_scale + 24.0 * math.log(2.0), log_scale)
        return latest * shrink, before * shrink, log_scale

    blank = jnp.zeros((2, X), jnp.float32)
    lax.fori_loop(0, M // 4, steps, (blank, blank, start_scale))
    for u in range(2):
        for lane in range(X // HALF):
            rows = table[lane, pl.ds(u, M, stride=2), :]
            high, low = split_pair(rows)
            upper[u, :, lane * HALF : (lane + 1) * HALF] = high
            lower[u, :, lane * HALF : (lane + 1) * HALF] = low


def legendre_pair(bin_index, lat_index):
    cos, log_sin, _, valid, log_norm = cycle_tables()
    first = bin_index + 32 * lat_index
    orders = jnp.stack([first, jnp.where(bin_index == 0, 496, 512) - first]).astype(jnp.int32)
    log_start = jnp.asarray(log_norm)[orders][:, None] + orders.astype(jnp.float32)[:, None] * log_sin
    start_scale = jnp.minimum(log_start, 0.0)
    diagonal = jnp.exp(log_start - start_scale) * valid
    degree = jnp.arange(M, dtype=jnp.int32)[None, :]
    degree_real = degree.astype(jnp.float32)
    lower_gap = degree - orders[:, None]
    upper_sum = degree + orders[:, None]
    inside = lower_gap > 0
    divisor = jnp.where(inside, lower_gap * upper_sum, 1).astype(jnp.float32)
    rise = jnp.sqrt((2.0 * degree_real + 1.0) * (2.0 * degree_real - 1.0) / divisor)
    fall = jnp.sqrt(
        (2.0 * degree_real + 1.0)
        * ((lower_gap - 1) * (upper_sum - 1)).astype(jnp.float32)
        / (jnp.maximum(2.0 * degree_real - 3.0, 1.0) * divisor)
    )
    rise = jnp.where(inside, rise, 0.0)
    fall = jnp.where(inside, fall, 0.0)
    smem = pl.BlockSpec(memory_space=pltpu.SMEM)
    vmem = pl.BlockSpec(memory_space=pltpu.VMEM)
    return pl.pallas_call(
        legendre_kernel,
        out_shape=[jax.ShapeDtypeStruct((2, M, X), jnp.bfloat16)] * 2,
        in_specs=[smem, smem, smem, vmem, vmem, vmem],
        out_specs=[vmem, vmem],
        scratch_shapes=[pltpu.VMEM((X // HALF, 2 * M, HALF), jnp.float32)],
        compiler_params=pltpu.CompilerParams(vmem_limit_bytes=48 * 2**20),
        cost_estimate=pl.CostEstimate(flops=10_000_000, bytes_accessed=1_600_000, transcendentals=0),
    )(orders, rise, fall, jnp.asarray(cos), diagonal, start_scale)


def dot(left, right):
    return jnp.dot(left, right, preferred_element_type=jnp.float32)


def twice(block):
    return jnp.concatenate([block, block], axis=0)


def block_kernel(
    fields, conv_weight, gain, support, upper, lower, one, two, three, four, weight,
    out,
    s1, g1, s2, g2, s3, g3, s4, g4, s5, g5, s6, g6, wide, pooled, convolved, near, far, send, recv,
):
    lat = lax.axis_index("lat")
    lon = lax.axis_index("lon")
    f32, bf16 = jnp.float32, jnp.bfloat16

    barrier = pltpu.get_barrier_semaphore()

    def greet_lon(step, _):
        pl.semaphore_signal(
            barrier, inc=1, device_id=(lat, (lon + step) % LON), device_id_type=MESH
        )
        return 0

    def greet_lat(step, _):
        pl.semaphore_signal(
            barrier, inc=1, device_id=((lat + step) % LAT, lon), device_id_type=MESH
        )
        return 0

    lax.fori_loop(1, LON, greet_lon, 0)
    lax.fori_loop(1, LAT, greet_lat, 0)
    pl.semaphore_wait(barrier, LON + LAT - 2)

    def send_lon(source, target, index):
        def one_peer(step, _):
            peer = (lon + step) % LON
            pltpu.make_async_remote_copy(
                src_ref=source.at[peer], dst_ref=target.at[lon], send_sem=send.at[index],
                recv_sem=recv.at[index], device_id=(lat, peer), device_id_type=MESH,
            ).start()
            return 0

        lax.fori_loop(1, LON, one_peer, 0)
        target[lon] = source[lon]

    def send_lat(source, target, index):
        def one_peer(step, _):
            peer = (lat + step) % LAT
            pltpu.make_async_remote_copy(
                src_ref=source.at[peer], dst_ref=target.at[lat], send_sem=send.at[index],
                recv_sem=recv.at[index], device_id=(peer, lon), device_id_type=MESH,
            ).start()
            return 0

        lax.fori_loop(1, LAT, one_peer, 0)
        target[lat] = source[lat]

    def whole(source, target, index, count):
        return pltpu.make_async_remote_copy(
            src_ref=source.at[pl.ds(0, count)], dst_ref=target.at[pl.ds(0, count)],
            send_sem=send.at[index], recv_sem=recv.at[index],
            device_id=((lat + 1) % LAT, (lon + 1) % LON), device_id_type=MESH,
        )

    for half in range(2):
        lanes = slice(half * HALF, (half + 1) * HALF)
        near[half, pl.ds(0, ROWS * COLS), :] = fields[:, :, lanes].astype(f32).reshape(ROWS * COLS, HALF)
        near[half, pl.ds(ROWS * COLS, COLS), :] = jnp.zeros((COLS, HALF), f32)

    def pack_residue(r, _):
        rows = [near[half, pl.ds(r, PAD, stride=COLS), :] for half in range(2)]
        s1[r] = jnp.concatenate(rows, axis=0).astype(bf16)
        return 0

    lax.fori_loop(0, LON, pack_residue, 0)
    send_lon(s1, g1, 0)

    halo_right = pltpu.make_async_remote_copy(
        src_ref=fields, dst_ref=wide.at[pl.ds(1, ROWS), pl.ds(0, COLS), :], send_sem=send.at[6],
        recv_sem=recv.at[6], device_id=(lat, (lon + 1) % LON), device_id_type=MESH,
    )
    halo_left = pltpu.make_async_remote_copy(
        src_ref=fields, dst_ref=wide.at[pl.ds(1, ROWS), pl.ds(2 * COLS, COLS), :],
        send_sem=send.at[7], recv_sem=recv.at[7], device_id=(lat, (lon + LON - 1) % LON),
        device_id_type=MESH,
    )
    halo_right.start()
    halo_left.start()
    wide[1 : ROWS + 1, COLS : 2 * COLS, :] = fields[...]

    whole(s1, g1, 0, LON - 1).wait_recv()
    far[...] = g1[...].astype(f32).reshape(LON * 2 * PAD, HALF)
    table = one[...]
    for group in range(6):
        block = jnp.concatenate(
            [far[pl.ds(group * 8 + n, 32, stride=48), :] for n in range(8)], axis=1
        ).astype(bf16)
        result = dot(table, twice(block))
        for n in range(8):
            half, row = divmod(group * 8 + n, PAD)
            lanes = slice(n * HALF, (n + 1) * HALF)
            for part in range(2):
                near[0, pl.ds(half * 48 + part * PAD + row, 16, stride=96), :] = result[
                    part * 16 : part * 16 + 16, lanes
                ]
    s2[...] = near[0].reshape(LON, 48, HALF).astype(bf16)
    send_lon(s2, g2, 1)

    halo_right.wait_recv()
    halo_left.wait_recv()
    halo_down = pltpu.make_async_remote_copy(
        src_ref=wide.at[ROWS], dst_ref=wide.at[0], send_sem=send.at[8], recv_sem=recv.at[8],
        device_id=((lat + 1) % LAT, lon), device_id_type=MESH,
    )
    halo_up = pltpu.make_async_remote_copy(
        src_ref=wide.at[1], dst_ref=wide.at[ROWS + 1], send_sem=send.at[9], recv_sem=recv.at[9],
        device_id=((lat + LAT - 1) % LAT, lon), device_id_type=MESH,
    )
    halo_down.start()
    halo_up.start()

    whole(s2, g2, 1, LON - 1).wait_recv()
    far[...] = g2[...].astype(f32).reshape(LON * 48, HALF)
    table = two[...]
    for group in range(3):
        block = jnp.concatenate(
            [
                jnp.concatenate(
                    [far[pl.ds(part * PAD + group * 8 + n, 32, stride=48), :] for part in range(2)],
                    axis=0,
                )
                for n in range(8)
            ],
            axis=1,
        ).astype(bf16)
        result = dot(table, twice(block))
        for n in range(8):
            row = group * 8 + n
            scaled = result[:, n * HALF : (n + 1) * HALF] * weight[pl.ds(row, 1), :]
            for k in range(4):
                near[0, pl.ds(k * PAD + row, 16, stride=96), :] = scaled[k * 16 : k * 16 + 16]
    s3[...] = near[0].reshape(LAT, 96, HALF).astype(bf16)
    send_lat(s3, g3, 2)

    halo_down.wait_recv()
    halo_up.wait_recv()
    halo_right.wait_send()
    halo_left.wait_send()
    halo_down.wait_send()
    halo_up.wait_send()
    edge = jnp.full((3 * COLS, 2 * HALF), lat, jnp.int32)
    wide[0] = jnp.where(edge > 0, wide[0].astype(f32), 0.0).astype(bf16)
    wide[ROWS + 1] = jnp.where(edge < LAT - 1, wide[ROWS + 1].astype(f32), 0.0).astype(bf16)
    source = lax.broadcasted_iota(jnp.int32, (COLS, 3 * COLS), 1)
    target = lax.broadcasted_iota(jnp.int32, (COLS, 3 * COLS), 0)
    offset = source - target - COLS
    offset_real = offset.astype(f32)
    distance = jnp.abs(offset)
    distance_real = distance.astype(f32)

    def pool(y, _):
        half_width = jnp.full((COLS, 3 * COLS), support[y], jnp.int32)
        span_len = (half_width + 1).astype(f32)
        inside = distance <= half_width
        triangle = jnp.where(inside, (span_len - distance_real) / span_len, 0.0)
        odd_basis = offset_real * triangle / span_len
        box_basis = jnp.where(inside, 1.0, 0.0) / jnp.sqrt(2.0 * half_width.astype(f32) + 1.0)
        band = jnp.concatenate([triangle, odd_basis, box_basis], axis=0).astype(bf16)
        start = pl.multiple_of(y * COLS, COLS)
        for a in range(3):
            basis = dot(band, wide[y + a]).astype(bf16)
            for k in range(3):
                pooled[pl.ds(start, COLS), pl.ds((a * 3 + k) * 256, 256)] = basis[
                    k * COLS : (k + 1) * COLS
                ]
        return 0

    lax.fori_loop(0, ROWS, pool, 0)

    whole(s3, g3, 2, LAT - 1).wait_recv()
    gains = jnp.concatenate([gain[...], gain[...]], axis=1)
    for u in range(2):
        data = jnp.concatenate(
            [
                g3[:, (2 * u + p) * PAD : (2 * u + p + 1) * PAD, :].astype(f32).reshape(X, HALF)
                for p in range(2)
            ],
            axis=1,
        ).astype(bf16)
        high, low = upper[u], lower[u]
        analysis = dot(high, data) + dot(low, data)
        filtered = (analysis * gains).astype(bf16)
        back = (((0,), (0,)), ((), ()))
        synthesis = lax.dot_general(
            high, filtered, back, preferred_element_type=f32
        ) + lax.dot_general(low, filtered, back, preferred_element_type=f32)
        for p in range(2):
            lanes = synthesis[:, p * HALF : (p + 1) * HALF].reshape(LAT, PAD, HALF)
            for a in range(LAT):
                near[1, pl.ds(a * 96 + (2 * u + p) * PAD, PAD), :] = lanes[a]
    s4[...] = near[1].reshape(LAT, 96, HALF).astype(bf16)
    send_lat(s4, g4, 3)

    rows = ROWS * COLS // 4
    for part in range(4):
        convolved[part * rows : (part + 1) * rows, :] = dot(
            pooled[part * rows : (part + 1) * rows, :], conv_weight[...]
        )

    whole(s4, g4, 3, LAT - 1).wait_recv()
    far[...] = g4[...].astype(f32).reshape(LAT * 96, HALF)
    table = three[...]
    for group in range(3):
        block = jnp.concatenate(
            [
                jnp.concatenate(
                    [far[pl.ds(k * PAD + group * 8 + n, 16, stride=96), :] for k in range(4)], axis=0
                )
                for n in range(8)
            ],
            axis=1,
        ).astype(bf16)
        result = dot(table, twice(block))
        for n in range(8):
            row = group * 8 + n
            for part in range(2):
                near[0, pl.ds(part * PAD + row, 32, stride=48), :] = result[
                    part * 32 : part * 32 + 32, n * HALF : (n + 1) * HALF
                ]
    s5[...] = near[0].reshape(LON, 48, HALF).astype(bf16)
    send_lon(s5, g5, 4)

    whole(s5, g5, 4, LON - 1).wait_recv()
    far[...] = g5[...].astype(f32).reshape(LON * 48, HALF)
    table = four[...]
    for group in range(6):
        block = jnp.concatenate(
            [
                jnp.concatenate(
                    [
                        far[
                            pl.ds(
                                (group * 8 + n) // PAD * 48 + part * PAD + (group * 8 + n) % PAD,
                                16, stride=96,
                            ),
                            :,
                        ]
                        for part in range(2)
                    ],
                    axis=0,
                )
                for n in range(8)
            ],
            axis=1,
        ).astype(bf16)
        result = dot(table, twice(block))
        for n in range(8):
            near[0, pl.ds(group * 8 + n, 32, stride=48), :] = result[
                :, n * HALF : (n + 1) * HALF
            ]
    s6[...] = near[0].reshape(LON, 48, HALF).astype(bf16)
    send_lon(s6, g6, 5)

    whole(s6, g6, 5, LON - 1).wait_recv()
    far[...] = g6[...].astype(f32).reshape(LON * 48, HALF)

    def finish(y, _):
        spectral = jnp.concatenate(
            [far[pl.ds(half * PAD + y, 32, stride=48), :] for half in range(2)], axis=1
        )
        start = pl.multiple_of(y * COLS, COLS)
        total = convolved[pl.ds(start, COLS), :] + spectral
        gelu = 0.5 * total * (1.0 + lax.erf(total * math.sqrt(0.5)))
        out[y] = (fields[y].astype(f32) + gelu).astype(bf16)
        return 0

    lax.fori_loop(0, ROWS, finish, 0)

    whole(s1, g1, 0, LON - 1).wait_send()
    whole(s2, g2, 1, LON - 1).wait_send()
    whole(s3, g3, 2, LAT - 1).wait_send()
    whole(s4, g4, 3, LAT - 1).wait_send()
    whole(s5, g5, 4, LON - 1).wait_send()
    whole(s6, g6, 5, LON - 1).wait_send()


def per_device(fields, conv_weight, spectral_gain, support):
    lat = lax.axis_index("lat")
    lon = lax.axis_index("lon")
    bin_index, half = lon // 2, lon % 2
    upper, lower = legendre_pair(bin_index, lat)
    one, two, three, four = longitude_tables()
    two = lax.dynamic_index_in_dim(jnp.asarray(two), bin_index, 0, keepdims=False)
    three = lax.dynamic_index_in_dim(jnp.asarray(three), bin_index, 0, keepdims=False)
    weight = lax.dynamic_index_in_dim(jnp.asarray(cycle_tables()[2]), lat, 0, keepdims=False)
    weight = jnp.broadcast_to(weight[:, None], (PAD, HALF))
    gain = lax.dynamic_slice_in_dim(spectral_gain, half * HALF, HALF, 1)
    vmem = pl.BlockSpec(memory_space=pltpu.VMEM)
    smem = pl.BlockSpec(memory_space=pltpu.SMEM)
    by_lon = pltpu.VMEM((LON, 48, HALF), jnp.bfloat16)
    by_lat = pltpu.VMEM((LAT, 96, HALF), jnp.bfloat16)
    return pl.pallas_call(
        block_kernel,
        out_shape=jax.ShapeDtypeStruct(fields.shape, fields.dtype),
        in_specs=[vmem, vmem, vmem, smem] + [vmem] * 7,
        out_specs=vmem,
        scratch_shapes=[by_lon] * 4
        + [by_lat] * 4
        + [by_lon] * 4
        + [
            pltpu.VMEM((ROWS + 2, 3 * COLS, 256), jnp.bfloat16),
            pltpu.VMEM((ROWS * COLS, 9 * 256), jnp.bfloat16),
            pltpu.VMEM((ROWS * COLS, 256), jnp.float32),
            pltpu.VMEM((2, LON * 48, HALF), jnp.float32),
            pltpu.VMEM((LON * 48, HALF), jnp.float32),
            pltpu.SemaphoreType.DMA((10,)),
            pltpu.SemaphoreType.DMA((10,)),
        ],
        compiler_params=pltpu.CompilerParams(
            collective_id=0, has_side_effects=True, vmem_limit_bytes=48 * 2**20
        ),
    )(
        fields, conv_weight.reshape(9 * 256, 256), gain, support, upper, lower,
        jnp.asarray(one), two, three, jnp.asarray(four), weight,
    )


def solution(mesh):
    placed = (P("lat", "lon", None), P(), P(), P("lat"))
    return jax.shard_map(
        per_device, mesh=mesh, in_specs=placed, out_specs=P("lat", "lon", None), check_vma=False
    )
```

time: 1740 us -> 117 us (0.07); the launches traced: 1710 us -> 116 us
  other arithmetic: 1060 us -> 1.05 us
  loops' own time: 339 us -> 0 us
  local copies, waits for them, and re-layouts: 185 us -> 4.72 us
  Pallas kernels: 0 us -> 110 us
  starting transfers between devices: 77.7 us -> 0 us
  matrix products: 27.5 us -> 0 us
  waiting for transfers between devices: 19.1 us -> 0 us
    sqrt x513 -> x0, other arithmetic: 657 us -> none  [the longest x256 328 us: recurrence(): jnp.sqrt(jnp.maximum((2.0 * degree_real + 1.0) * ((lower_gap - 1) * (uppe...]
    another operation x1 -> x0, loops' own time: 339 us -> none  [legendre_table(): lax.scan(recurrence, (blank, blank, blank), jnp.arange(degrees, dtype=jnp...]
    eq x512 -> x0, other arithmetic: 329 us -> none  [recurrence(): current = jnp.where(lower_gap == 0, diagonal_start, current)]
    pallas_call x0 -> x2, Pallas kernels: none -> 110 us  [the longest x1 106 us: per_device(): pl.pallas_call(block_kernel, out_shape=jax.ShapeDtypeStruct(fields.shape,...]
    all_to_all x6 -> x0, starting transfers between devices: 57.8 us -> none  [the longest x1 14.3 us: per_device(): lax.all_to_all(fields, 'lon', split_axis=2, concat_axis=1, tiled=True)]
    convert_element_type x13 -> x0, local copies, waits for them, and re-layouts: 56.1 us -> none  [the longest x4 19.8 us: split_pair(): upper_part = table.astype(jnp.bfloat16)]
    while x496 -> x0, other arithmetic: 47 us -> none
    unnamed x45 -> x15, local copies, waits for them, and re-layouts: 43.9 us -> 1.76 us
  transfers between devices with their start and end apart: 10 -> 0, of which waited for: 2 -> 0; matrix products, arithmetic and copies ran while one was open for 69% -> 0% of each run, Pallas kernels for 0% -> 0%
where the time goes in v1:
time: 117 us; the launch traced here: 116 us
  Pallas kernels  110 us (94%)
  local copies, waits for them, and re-layouts  4.72 us (4%)
    pallas_call x1, Pallas kernels, per_device(): pl.pallas_call(block_kernel, out_shape=jax.ShapeDtypeStruct(fields.shape,...  106 us
    pallas_call x1, Pallas kernels, legendre_pair(): pl.pallas_call(legendre_kernel, out_shape=[jax.ShapeDtypeStruct((2, M, X)...  4.71 us

profile of v1, /device:TPU:1, one launch (start us, length us, event | category | flops | bytes accessed | tf_op | source)
XLA Modules:
  0.0 116.4 jit_solution(4275277745929641637)
XLA Ops:
  0.0 0.0 copy-start
  0.0 0.0 copy-start.6
  0.0 0.0 copy-start.3
  0.0 0.0 copy-start.4
  0.0 0.0 copy-start.5
  0.0 0.0 copy-start.1
  0.1 0.8 fusion.2
  0.9 0.1 fusion.3
  1.0 0.1 fusion.4
  1.1 1.3 %gather_fusion = f32[2]{0:T(128)S(1)} fusion(f32[512]{0:T(512)} %constant.92.clone, s32[1024]{0:T(1024)S(1)} %pad_clamp_fusion), kind=kCustom, calls=%fused_computation | custom fusion | bytes 24 | tf_op jit(solution)/shard_map/gather | solution.py:149
  2.4 0.1 sqrt_select_fusion
  2.5 0.8 fusion
  3.3 0.1 broadcast_in_dim.26.weight
  3.3 0.7 dynamic-slice_bitcast_fusion
  4.1 0.0 copy-done
  4.1 0.0 copy-done.6
  4.1 4.7 %shard_map.127 = (bf16[2,512,384]{2,1,0:T(8,128)(2,1)S(1)}, bf16[2,512,384]{2,1,0:T(8,128)(2,1)S(1)}) custom-call(s32[2]{0:T(128)S(1)} %get-tuple-element.10.orders, f32[2,512]{1,0:T(2,128)S(1)} %get-tuple-element.14.rise, f32[2,512]{1,0:T(2,128)S(1)} %get-tuple-element.13.fall, f32[1,384]{1,0:T(1,128)S(1)} %copy-done.6, ...), custom_call_target="tpu_custom_call" | custom-call | flops 10000000 | bytes 1600000 | tf_op jit(solution)/shard_map/pallas_call | solution.py:168
  8.8 0.0 copy-done.3
  8.8 0.0 copy-done.4
  8.9 0.0 copy-done.5
  8.9 0.0 copy-done.1
  8.9 0.0 copy-start.2
  8.9 1.0 copy-done.2
  9.9 105.8 %shard_map.128 = bf16[23,32,256]{2,1,0:T(8,128)(2,1)S(1)} custom-call(bf16[23,32,256]{2,1,0:T(8,128)(2,1)S(1)} %copy-done.2, bf16[2304,256]{1,0:T(8,128)(2,1)S(1)} %bitcast.13, f32[512,128]{1,0:T(8,128)S(1)} %constant_dynamic-slice_fusion.1.gain, s32[23]{0:T(128)S(1)} %copy-done.5, bf16[2,512,384]{2,1,0:T(8,128)(2,1)S(1)} %get-tuple-element.7.upper, ...), custom_call_target="tpu_custom_call" | custom-call | tf_op jit(solution)/shard_map/pallas_call | solution.py:482
  115.6 0.7 copy.15
  (4 shorter events, 0.0 us)
Async XLA Ops:
  0.0 4.1 %copy-start = (f32[512,256]{1,0:T(8,128)S(1)}, f32[512,256]{1,0:T(8,128)}, u32[]{:S(2)}) copy-start(f32[512,256]{1,0:T(8,128)} %param.15) | copy-start | bytes 1572868
  0.0 4.1 %copy-start.6 = (f32[1,384]{1,0:T(1,128)S(1)}, f32[1,384]{1,0:T(1,128)}, u32[]{:S(2)}) copy-start(f32[1,384]{1,0:T(1,128)} %constant.95.clone.cos_ref) | copy-start | bytes 4612
  0.0 8.8 %copy-start.3 = (bf16[32,64]{1,0:T(8,128)(2,1)S(1)}, bf16[32,64]{1,0:T(8,128)(2,1)}, u32[]{:S(2)}) copy-start(bf16[32,64]{1,0:T(8,128)(2,1)} %constant.100.clone.four) | copy-start | bytes 12292
  0.0 8.8 %copy-start.4 = (bf16[32,64]{1,0:T(8,128)(2,1)S(1)}, bf16[32,64]{1,0:T(8,128)(2,1)}, u32[]{:S(2)}) copy-start(bf16[32,64]{1,0:T(8,128)(2,1)} %constant.99.clone.one) | copy-start | bytes 12292
  0.0 8.8 %copy-start.5 = (s32[23]{0:T(128)S(1)}, s32[23]{0:T(128)}, u32[]{:S(2)}) copy-start(s32[23]{0:T(128)} %support.1) | copy-start | bytes 280
  0.0 8.8 %copy-start.1 = (bf16[3,3,256,256]{3,2,1,0:T(8,128)(2,1)S(1)}, bf16[3,3,256,256]{3,2,1,0:T(8,128)(2,1)}, u32[]{:S(2)}) copy-start(bf16[3,3,256,256]{3,2,1,0:T(8,128)(2,1)} %param.14) | copy-start | bytes 3538948
  8.9 1.0 copy-start.2

commit v2 on v1

v2 whole, which is shorter than its diff:
```python
import functools
import math

import jax
import jax.numpy as jnp
import numpy as np
from jax import lax
from jax.experimental import pallas as pl
from jax.experimental.pallas import tpu as pltpu
from jax.sharding import PartitionSpec as P

NLAT = 368
NLON = 1024
M = 512
SMAX = 24
LAT = 16
LON = 32
ROWS = 23
PAD = 24
COLS = 32
HALF = 128
X = LAT * PAD
MESH = pl.DeviceIdType.MESH


def split_pair(table):
    upper_part = table.astype(jnp.bfloat16)
    lower_part = (table - upper_part.astype(jnp.float32)).astype(jnp.bfloat16)
    return upper_part, lower_part


def doubled(table):
    upper = table.astype(jnp.bfloat16)
    lower = (table - upper.astype(np.float32)).astype(jnp.bfloat16)
    return np.concatenate([upper, lower], axis=-1)


def orders_of(bin_index, lat_index):
    first = bin_index + 32 * lat_index
    second = (496 if bin_index == 0 else 512) - first
    return first, second


@functools.lru_cache
def longitude_tables():
    turn = 2.0 * np.pi / NLON
    b = np.arange(32)
    step_one = np.zeros((2, 16, 32))
    for q in range(16):
        step_one[0, q] = np.cos(2 * np.pi * b * q / 32)
        step_one[1, q] = np.sin(2 * np.pi * b * q / 32) if q else (-1.0) ** b
    step_one = step_one.reshape(32, 32)
    r = np.arange(32)
    step_two = np.zeros((16, 2, 2, 16, 2, 32))
    weight = np.zeros((16, 2, 2, 16))
    for q in range(16):
        for a in range(16):
            for u, m in enumerate(orders_of(q, a)):
                cos, sin = np.cos(turn * ((m * r) % NLON)), np.sin(turn * ((m * r) % NLON))
                weight[q, u, :, a] = 1.0 if m == 0 else 2.0
                if q == 0:
                    step_two[q, u, 0, a, u] = cos
                    step_two[q, u, 1, a, u] = sin
                else:
                    sign = 1.0 if u == 0 else -1.0
                    step_two[q, u, 0, a, 0] = cos
                    step_two[q, u, 0, a, 1] = -sign * sin
                    step_two[q, u, 1, a, 0] = sin
                    step_two[q, u, 1, a, 1] = sign * cos
    step_two = step_two.reshape(16, 2, 2, 8, 2, 64).transpose(0, 2, 4, 1, 3, 5).reshape(16, 64, 64)
    weight = weight.reshape(16, 2, 2, 8, 2).transpose(0, 2, 4, 1, 3).reshape(16, 64, 1)
    back = np.swapaxes(step_two * weight, 1, 2)
    f32 = np.float32
    return (
        doubled(step_one.astype(f32)),
        doubled((step_two / NLON).astype(f32)),
        doubled(back.astype(f32)),
        doubled(step_one.T.astype(f32)),
    )


@functools.lru_cache
def cycle_tables():
    t = np.pi * (np.arange(NLAT) + 0.5) / NLAT
    f32 = np.float32

    def placed(values):
        padded = np.zeros((LAT, PAD))
        padded[:, :ROWS] = values.reshape(LAT, ROWS)
        return padded.reshape(4, 2, 2, PAD).transpose(0, 2, 1, 3).astype(f32)

    weight = placed(np.sin(t) * np.pi / NLAT).reshape(8, 2, PAD).transpose(0, 2, 1)
    weight = np.repeat(weight, 64, axis=2)
    k = np.arange(1, M)
    log_norm = np.concatenate([[0.0], np.cumsum(np.log((2 * k - 1) / (2 * k)))])
    log_norm = 0.5 * np.log((2 * np.arange(M) + 1) / 2) + 0.5 * log_norm
    rows = np.stack(
        [placed(np.cos(t)).reshape(X), placed(np.log(np.sin(t))).reshape(X), placed(np.ones(NLAT)).reshape(X)]
    )
    return rows, weight, log_norm.reshape(1, M).astype(f32)


def dot(left, right):
    return jnp.dot(left, right, preferred_element_type=jnp.float32)


def twice(block):
    return jnp.concatenate([block, block], axis=0)


def trade(first, second):
    low = lax.broadcasted_iota(jnp.int32, first.shape, 1) < 64
    return (
        jnp.where(low, first, pltpu.roll(second, 64, axis=1)),
        jnp.where(low, pltpu.roll(first, 64, axis=1), second),
    )


def legendre_orders(bin_index, owner, cycle_rows, log_norm, up_table, down_table, table, legendre):
    f32 = jnp.float32

    def order_rows(slot):
        first = bin_index + 64 * owner + 32 * (slot // 2)
        return jnp.where(slot % 2 == 0, first, jnp.where(bin_index == 0, 496, 512) - first)

    def coefficients(block, _):
        row = lax.broadcasted_iota(jnp.int32, (128, HALF), 0)
        degree = (block * 32 + row // 4).astype(f32)
        order = order_rows(row % 4).astype(f32)
        gap, total = degree - order, degree + order
        inside = gap > 0.5
        odd = 2.0 * degree + 1.0
        shared = odd / jnp.where(inside, gap * total, 1.0)
        rise = jnp.sqrt(shared * jnp.maximum(2.0 * degree - 1.0, 0.0))
        fall = jnp.sqrt(
            shared * jnp.maximum((gap - 1.0) * (total - 1.0), 0.0) / jnp.maximum(2.0 * degree - 3.0, 1.0)
        )
        start = pl.multiple_of(block * 128, 128)
        up_table[pl.ds(start, 128), :] = jnp.where(inside, rise, 0.0)
        down_table[pl.ds(start, 128), :] = jnp.where(inside, fall, 0.0)
        return 0

    lax.fori_loop(0, 16, coefficients, 0)
    order = order_rows(lax.broadcasted_iota(jnp.int32, (4, X), 0))
    wide_order = order_rows(lax.broadcasted_iota(jnp.int32, (4, M), 0))
    column = lax.broadcasted_iota(jnp.int32, (4, M), 1)
    norm = jnp.sum(jnp.where(column == wide_order, log_norm[...], 0.0), axis=1, keepdims=True)
    cosines = jnp.broadcast_to(cycle_rows[pl.ds(0, 1), :], (4, X))
    log_start = norm + order.astype(f32) * cycle_rows[pl.ds(1, 1), :]
    start_scale = jnp.minimum(log_start, 0.0)
    diagonal = jnp.exp(log_start - start_scale) * cycle_rows[pl.ds(2, 1), :]

    def spread(rows):
        return jnp.concatenate([rows] * (X // HALF), axis=1)

    def steps(block, state):
        latest, before, log_scale = state
        factor = jnp.exp(log_scale)
        for k in range(4):
            degree = block * 4 + k
            up = spread(up_table[pl.ds(4 * degree, 4), :]) * cosines
            down = spread(down_table[pl.ds(4 * degree, 4), :])
            current = up * latest + (jnp.where(order == degree, diagonal, 0.0) - down * before)
            value = current * factor
            for lane in range(X // HALF):
                table[lane, pl.ds(4 * degree, 4), :] = value[:, lane * HALF : (lane + 1) * HALF]
            latest, before = current, latest
        too_big = jnp.abs(latest) > 2.0**24
        shrink = jnp.where(too_big, 2.0**-24, 1.0)
        log_scale = jnp.where(too_big, log_scale + 24.0 * math.log(2.0), log_scale)
        return latest * shrink, before * shrink, log_scale

    blank = jnp.zeros((4, X), f32)
    lax.fori_loop(0, M // 4, steps, (blank, blank, start_scale))
    for slot in range(4):
        for lane in range(X // HALF):
            legendre[slot, :, lane * HALF : (lane + 1) * HALF] = table[
                lane, pl.ds(slot, M, stride=4), :
            ].astype(jnp.bfloat16)


def block_kernel(
    fields, conv_weight, gain, support, one, two, three, four, cycle_rows, weight, log_norm,
    out,
    s1, g1, s2, g2, s3, g3, s4, g4, s5, g5, s6, g6, wide, pooled, convolved, near, far,
    up_table, down_table, table, legendre, gains, send, recv,
):
    lat = lax.axis_index("lat")
    lon = lax.axis_index("lon")
    hemi = lat // 2 % 2
    owner = lat // 4 * 2 + lat % 2
    spot = hemi * LON + lon
    bin_index, half_index = lon // 2, lon % 2
    f32, bf16 = jnp.float32, jnp.bfloat16

    def double_peer(step):
        index = (spot + step) % (2 * LON)
        return index, (lat // 4 * 4 + index // LON * 2 + lat % 2, index % LON)

    def owner_peer(step):
        index = (owner + step) % 8
        return index, (index // 2 * 4 + hemi * 2 + index % 2, lon)

    def ring_peer(step):
        index = (lon + step) % LON
        return index, (lat, index)

    barrier = pltpu.get_barrier_semaphore()

    def greet(peer_of):
        def one_peer(step, _):
            pl.semaphore_signal(barrier, inc=1, device_id=peer_of(step)[1], device_id_type=MESH)
            return 0

        return one_peer

    lax.fori_loop(1, 2 * LON, greet(double_peer), 0)
    lax.fori_loop(1, 8, greet(owner_peer), 0)
    for step in (1, LAT - 1):
        pl.semaphore_signal(
            barrier, inc=1, device_id=((lat + step) % LAT, lon), device_id_type=MESH
        )

    def exchange(source, target, index, peer_of, mine, count):
        def one_peer(step, _):
            peer, device = peer_of(step)
            pltpu.make_async_remote_copy(
                src_ref=source.at[peer], dst_ref=target.at[mine], send_sem=send.at[index],
                recv_sem=recv.at[index], device_id=device, device_id_type=MESH,
            ).start()
            return 0

        lax.fori_loop(1, count, one_peer, 0)
        target[mine] = source[mine]

    def whole(source, target, index, count):
        return pltpu.make_async_remote_copy(
            src_ref=source.at[pl.ds(0, count)], dst_ref=target.at[pl.ds(0, count)],
            send_sem=send.at[index], recv_sem=recv.at[index],
            device_id=(lat, (lon + 1) % LON), device_id_type=MESH,
        )

    for half in range(2):
        lanes = slice(half * HALF, (half + 1) * HALF)
        near[half, pl.ds(0, ROWS * COLS), :] = fields[:, :, lanes].astype(f32).reshape(ROWS * COLS, HALF)
        near[half, pl.ds(ROWS * COLS, COLS), :] = jnp.zeros((COLS, HALF), f32)

    def pack_residue(r, _):
        rows = [near[half, pl.ds(r, PAD, stride=COLS), :] for half in range(2)]
        s1[r] = jnp.concatenate(rows, axis=0).astype(bf16)
        return 0

    lax.fori_loop(0, LON, pack_residue, 0)
    pl.semaphore_wait(barrier, 2 * LON - 1 + 7 + 2)
    exchange(s1, g1, 0, ring_peer, lon, LON)

    legendre_orders(
        bin_index, owner, cycle_rows, log_norm, up_table, down_table, table, legendre
    )
    own_gain = gain[:, pl.ds(pl.multiple_of(half_index * HALF, HALF), HALF)]
    turned = pltpu.roll(own_gain, 64, axis=1)
    lower_lanes = lax.broadcasted_iota(jnp.int32, (M, HALF), 1) // 64
    gains[...] = jnp.where(lower_lanes == hemi, own_gain, turned)
    wide[1 : ROWS + 1, COLS : 2 * COLS, :] = fields[...]

    whole(s1, g1, 0, LON - 1).wait_recv()
    far[...] = g1[...].astype(f32).reshape(LON * 48, HALF)
    matrix = one[...]
    for group in range(6):
        block = jnp.concatenate(
            [far[pl.ds(group * 8 + n, 32, stride=48), :] for n in range(8)], axis=1
        ).astype(bf16)
        result = dot(matrix, twice(block))
        for n in range(8):
            half, row = divmod(group * 8 + n, PAD)
            lanes = slice(n * HALF, (n + 1) * HALF)
            quarters = trade(result[0:16, lanes], result[16:32, lanes])
            for g in range(2):
                near[0, pl.ds((g * LON + half) * PAD + row, 16, stride=48), :] = quarters[g]
    s2[...] = near[0].reshape(2 * LON, PAD, HALF).astype(bf16)
    exchange(s2, g2, 1, double_peer, spot, 2 * LON)

    halo_right = pltpu.make_async_remote_copy(
        src_ref=fields, dst_ref=wide.at[pl.ds(1, ROWS), pl.ds(0, COLS), :], send_sem=send.at[6],
        recv_sem=recv.at[6], device_id=(lat, (lon + 1) % LON), device_id_type=MESH,
    )
    halo_left = pltpu.make_async_remote_copy(
        src_ref=fields, dst_ref=wide.at[pl.ds(1, ROWS), pl.ds(2 * COLS, COLS), :],
        send_sem=send.at[7], recv_sem=recv.at[7], device_id=(lat, (lon + LON - 1) % LON),
        device_id_type=MESH,
    )

    whole(s2, g2, 1, 2 * LON - 1).wait_recv()
    halo_right.start()
    halo_left.start()
    far[...] = g2[...].astype(f32).reshape(2 * LON * PAD, HALF)
    matrix = two[bin_index]
    weights = weight[owner]
    for group in range(3):
        columns = []
        for n in range(8):
            row = group * 8 + n
            columns.append(
                jnp.concatenate(
                    trade(
                        far[pl.ds(row, 32, stride=PAD), :],
                        far[pl.ds(LON * PAD + row, 32, stride=PAD), :],
                    ),
                    axis=0,
                )
            )
        result = dot(matrix, twice(jnp.concatenate(columns, axis=1).astype(bf16)))
        for n in range(8):
            row = group * 8 + n
            scaled = result[:, n * HALF : (n + 1) * HALF] * weights[row : row + 1, :]
            sides = trade(scaled[0:32], scaled[32:64])
            for g in range(2):
                for slot in range(4):
                    near[0, pl.ds(slot * 48 + g * PAD + row, 8, stride=192), :] = sides[g][
                        slot * 8 : slot * 8 + 8
                    ]
    s3[...] = near[0].reshape(8, 192, HALF).astype(bf16)
    exchange(s3, g3, 2, owner_peer, owner, 8)

    whole(s3, g3, 2, 7).wait_recv()
    for slot in range(4):
        data = g3[:, slot * 48 : slot * 48 + 48, :].reshape(X, HALF)
        filtered = (dot(legendre[slot], data) * gains[...]).astype(bf16)
        synthesis = lax.dot_general(
            legendre[slot], filtered, (((0,), (0,)), ((), ())), preferred_element_type=f32
        )
        s4[:, slot * 48 : slot * 48 + 48, :] = synthesis.reshape(8, 48, HALF).astype(bf16)
    exchange(s4, g4, 3, owner_peer, owner, 8)

    halo_right.wait_recv()
    halo_left.wait_recv()
    halo_down = pltpu.make_async_remote_copy(
        src_ref=wide.at[ROWS], dst_ref=wide.at[0], send_sem=send.at[8], recv_sem=recv.at[8],
        device_id=((lat + 1) % LAT, lon), device_id_type=MESH,
    )
    halo_up = pltpu.make_async_remote_copy(
        src_ref=wide.at[1], dst_ref=wide.at[ROWS + 1], send_sem=send.at[9], recv_sem=recv.at[9],
        device_id=((lat + LAT - 1) % LAT, lon), device_id_type=MESH,
    )
    halo_down.start()
    halo_up.start()

    whole(s4, g4, 3, 7).wait_recv()
    far[...] = g4[...].astype(f32).reshape(8 * 192, HALF)
    matrix = three[bin_index]
    for group in range(3):
        columns = []
        for n in range(8):
            row = group * 8 + n
            sides = [
                jnp.concatenate(
                    [
                        far[pl.ds(slot * 48 + g * PAD + row, 8, stride=192), :]
                        for slot in range(4)
                    ],
                    axis=0,
                )
                for g in range(2)
            ]
            columns.append(jnp.concatenate(trade(*sides), axis=0))
        result = dot(matrix, twice(jnp.concatenate(columns, axis=1).astype(bf16)))
        for n in range(8):
            row = group * 8 + n
            lanes = slice(n * HALF, (n + 1) * HALF)
            sides = trade(result[0:32, lanes], result[32:64, lanes])
            for g in range(2):
                near[0, pl.ds(g * LON * PAD + row, 32, stride=PAD), :] = sides[g]
    s5[...] = near[0].reshape(2 * LON, PAD, HALF).astype(bf16)
    exchange(s5, g5, 4, double_peer, spot, 2 * LON)

    halo_down.wait_recv()
    halo_up.wait_recv()
    halo_right.wait_send()
    halo_left.wait_send()
    halo_down.wait_send()
    halo_up.wait_send()
    edge = jnp.full((3 * COLS, 2 * HALF), lat, jnp.int32)
    wide[0] = jnp.where(edge > 0, wide[0].astype(f32), 0.0).astype(bf16)
    wide[ROWS + 1] = jnp.where(edge < LAT - 1, wide[ROWS + 1].astype(f32), 0.0).astype(bf16)
    source = lax.broadcasted_iota(jnp.int32, (COLS, 3 * COLS), 1)
    target = lax.broadcasted_iota(jnp.int32, (COLS, 3 * COLS), 0)
    offset = source - target - COLS
    offset_real = offset.astype(f32)
    distance = jnp.abs(offset)
    distance_real = distance.astype(f32)

    def pool(y, _):
        half_width = jnp.full((COLS, 3 * COLS), support[y], jnp.int32)
        span_len = (half_width + 1).astype(f32)
        inside = distance <= half_width
        triangle = jnp.where(inside, (span_len - distance_real) / span_len, 0.0)
        odd_basis = offset_real * triangle / span_len
        box_basis = jnp.where(inside, 1.0, 0.0) / jnp.sqrt(2.0 * half_width.astype(f32) + 1.0)
        band = jnp.concatenate([triangle, odd_basis, box_basis], axis=0).astype(bf16)
        start = pl.multiple_of(y * COLS, COLS)
        for a in range(3):
            basis = dot(band, wide[y + a]).astype(bf16)
            for k in range(3):
                pooled[pl.ds(start, COLS), pl.ds((a * 3 + k) * 256, 256)] = basis[
                    k * COLS : (k + 1) * COLS
                ]
        return 0

    lax.fori_loop(0, ROWS, pool, 0)

    whole(s5, g5, 4, 2 * LON - 1).wait_recv()
    far[...] = g5[...].astype(f32).reshape(2 * LON * PAD, HALF)
    matrix = four[...]
    for group in range(6):
        columns = []
        for n in range(8):
            half, row = divmod(group * 8 + n, PAD)
            columns.append(
                jnp.concatenate(
                    trade(
                        far[pl.ds(half * PAD + row, 16, stride=48), :],
                        far[pl.ds((LON + half) * PAD + row, 16, stride=48), :],
                    ),
                    axis=0,
                )
            )
        result = dot(matrix, twice(jnp.concatenate(columns, axis=1).astype(bf16)))
        for n in range(8):
            near[0, pl.ds(group * 8 + n, 32, stride=48), :] = result[
                :, n * HALF : (n + 1) * HALF
            ]
    s6[...] = near[0].reshape(LON, 48, HALF).astype(bf16)
    exchange(s6, g6, 5, ring_peer, lon, LON)

    rows = ROWS * COLS // 4
    for part in range(4):
        convolved[part * rows : (part + 1) * rows, :] = dot(
            pooled[part * rows : (part + 1) * rows, :], conv_weight[...]
        )

    whole(s6, g6, 5, LON - 1).wait_recv()
    far[...] = g6[...].astype(f32).reshape(LON * 48, HALF)

    def finish(y, _):
        spectral = jnp.concatenate(
            [far[pl.ds(half * PAD + y, 32, stride=48), :] for half in range(2)], axis=1
        )
        start = pl.multiple_of(y * COLS, COLS)
        total = convolved[pl.ds(start, COLS), :] + spectral
        gelu = 0.5 * total * (1.0 + lax.erf(total * math.sqrt(0.5)))
        out[y] = (fields[y].astype(f32) + gelu).astype(bf16)
        return 0

    lax.fori_loop(0, ROWS, finish, 0)

    whole(s1, g1, 0, LON - 1).wait_send()
    whole(s2, g2, 1, 2 * LON - 1).wait_send()
    whole(s3, g3, 2, 7).wait_send()
    whole(s4, g4, 3, 7).wait_send()
    whole(s5, g5, 4, 2 * LON - 1).wait_send()
    whole(s6, g6, 5, LON - 1).wait_send()


def per_device(fields, conv_weight, spectral_gain, support):
    vmem = pl.BlockSpec(memory_space=pltpu.VMEM)
    smem = pl.BlockSpec(memory_space=pltpu.SMEM)
    by_ring = pltpu.VMEM((LON, 48, HALF), jnp.bfloat16)
    by_double = pltpu.VMEM((2 * LON, PAD, HALF), jnp.bfloat16)
    by_owner = pltpu.VMEM((8, 192, HALF), jnp.bfloat16)
    tables = longitude_tables() + cycle_tables()
    return pl.pallas_call(
        block_kernel,
        out_shape=jax.ShapeDtypeStruct(fields.shape, fields.dtype),
        in_specs=[vmem, vmem, vmem, smem] + [vmem] * 7,
        out_specs=vmem,
        scratch_shapes=[by_ring] * 2
        + [by_double] * 2
        + [by_owner] * 4
        + [by_double] * 2
        + [by_ring] * 2
        + [
            pltpu.VMEM((ROWS + 2, 3 * COLS, 256), jnp.bfloat16),
            pltpu.VMEM((ROWS * COLS, 9 * 256), jnp.bfloat16),
            pltpu.VMEM((ROWS * COLS, 256), jnp.float32),
            pltpu.VMEM((2, LON * 48, HALF), jnp.float32),
            pltpu.VMEM((LON * 48, HALF), jnp.float32),
            pltpu.VMEM((4 * M, HALF), jnp.float32),
            pltpu.VMEM((4 * M, HALF), jnp.float32),
            pltpu.VMEM((X // HALF, 4 * M, HALF), jnp.float32),
            pltpu.VMEM((4, M, X), jnp.bfloat16),
            pltpu.VMEM((M, HALF), jnp.float32),
            pltpu.SemaphoreType.DMA((10,)),
            pltpu.SemaphoreType.DMA((10,)),
        ],
        compiler_params=pltpu.CompilerParams(
            collective_id=0, has_side_effects=True, vmem_limit_bytes=48 * 2**20
        ),
    )(
        fields, conv_weight.reshape(9 * 256, 256), spectral_gain, support,
        *[jnp.asarray(table) for table in tables],
    )


def solution(mesh):
    placed = (P("lat", "lon", None), P(), P(), P("lat"))
    return jax.shard_map(
        per_device, mesh=mesh, in_specs=placed, out_specs=P("lat", "lon", None), check_vma=False
    )
```

time: 117 us -> 96.9 us (0.83)
  Pallas kernels: 110 us -> 85.5 us
  local copies, waits for them, and re-layouts: 4.72 us -> 10.3 us
    pallas_call x1, Pallas kernels: 106 us -> 85.5 us  [per_device(): pl.pallas_call(block_kernel, out_shape=jax.ShapeDtypeStruct(fields.shape,...]
    unnamed x15 -> x23, local copies, waits for them, and re-layouts: 1.76 us -> 10.3 us
    pallas_call x1 -> x0, Pallas kernels: 4.71 us -> none  [legendre_pair(): pl.pallas_call(legendre_kernel, out_shape=[jax.ShapeDtypeStruct((2, M, X)...]
    gather x1 -> x0, local copies, waits for them, and re-layouts: 1.32 us -> none  [legendre_pair(): jnp.asarray(log_norm)[orders][:, None]]
where the time goes in v2:
time: 96.9 us; the launch traced here: 95.8 us
  Pallas kernels  85.5 us (88%)
  local copies, waits for them, and re-layouts  10.3 us (11%)
    pallas_call x1, Pallas kernels, per_device(): pl.pallas_call(block_kernel, out_shape=jax.ShapeDtypeStruct(fields.shape,...  85.5 us
    unnamed x23, local copies, waits for them, and re-layouts  10.3 us

profile of v2, /device:TPU:1, one launch (start us, length us, event | category | flops | bytes accessed | tf_op | source)
XLA Modules:
  0.0 95.8 jit_solution(9413806220508136386)
XLA Ops:
  0.0 0.0 copy-start
  0.0 1.3 %copy-done = bf16[3,3,256,256]{3,2,1,0:T(8,128)(2,1)S(1)} copy-done((bf16[3,3,256,256]{3,2,1,0:T(8,128)(2,1)S(1)}, bf16[3,3,256,256]{3,2,1,0:T(8,128)(2,1)}, u32[]{:S(2)}) %copy-start) | copy-done | bytes 1179672
  1.3 0.0 copy-start.1
  1.3 1.0 %copy-done.1 = f32[512,256]{1,0:T(8,128)S(1)} copy-done((f32[512,256]{1,0:T(8,128)S(1)}, f32[512,256]{1,0:T(8,128)}, u32[]{:S(2)}) %copy-start.1) | copy-done | bytes 524312
  2.3 0.0 copy-start.2
  2.3 1.0 %copy-done.2 = bf16[23,32,256]{2,1,0:T(8,128)(2,1)S(1)} copy-done((bf16[23,32,256]{2,1,0:T(8,128)(2,1)S(1)}, bf16[23,32,256]{2,1,0:T(8,128)(2,1)}, u32[]{:S(2)}) %copy-start.2) | copy-done | bytes 376856
  3.3 0.0 copy-start.3
  3.3 0.9 copy-done.3
  4.3 0.0 copy-start.4
  4.3 0.9 copy-done.4
  5.2 0.0 copy-start.5
  5.2 0.9 copy-done.5
  6.1 0.0 copy-start.6
  6.1 0.7 copy-done.6
  6.8 0.0 copy-start.7
  6.8 0.7 copy-done.7
  7.5 0.0 copy-start.8
  7.5 0.7 copy-done.8
  8.2 0.0 copy-start.9
  8.2 0.7 copy-done.9
  8.9 0.0 copy-start.10
  8.9 0.7 copy-done.10
  9.5 85.5 %shard_map.109 = bf16[23,32,256]{2,1,0:T(8,128)(2,1)S(1)} custom-call(bf16[23,32,256]{2,1,0:T(8,128)(2,1)S(1)} %copy-done.2, bf16[2304,256]{1,0:T(8,128)(2,1)S(1)} %bitcast.1, f32[512,256]{1,0:T(8,128)S(1)} %copy-done.1, s32[23]{0:T(128)S(1)} %copy-done.10, bf16[32,64]{1,0:T(8,128)(2,1)S(1)} %copy-done.7, bf16[16,64,128]{2,1,0:T(8,128)(2,1)S(1)} %copy-done.4, ...), custom_call_target="tpu_custom_call" | custom-call | tf_op jit(solution)/shard_map/pallas_call | solution.py:471
  95.0 0.7 copy.13
Async XLA Ops:
  0.0 1.3 %copy-start = (bf16[3,3,256,256]{3,2,1,0:T(8,128)(2,1)S(1)}, bf16[3,3,256,256]{3,2,1,0:T(8,128)(2,1)}, u32[]{:S(2)}) copy-start(bf16[3,3,256,256]{3,2,1,0:T(8,128)(2,1)} %param.12) | copy-start | bytes 3538948
  1.3 1.0 %copy-start.1 = (f32[512,256]{1,0:T(8,128)S(1)}, f32[512,256]{1,0:T(8,128)}, u32[]{:S(2)}) copy-start(f32[512,256]{1,0:T(8,128)} %gain.1) | copy-start | bytes 1572868
  2.3 1.0 %copy-start.2 = (bf16[23,32,256]{2,1,0:T(8,128)(2,1)S(1)}, bf16[23,32,256]{2,1,0:T(8,128)(2,1)}, u32[]{:S(2)}) copy-start(bf16[23,32,256]{2,1,0:T(8,128)(2,1)} %fields.1) | copy-start | bytes 1130500
  3.3 0.9 copy-start.3
  4.3 0.9 copy-start.4
  5.2 0.9 copy-start.5
  6.1 0.7 copy-start.6
  6.8 0.7 copy-start.7
  7.5 0.7 copy-start.8
  8.2 0.7 copy-start.9
  8.9 0.7 copy-start.10

commit v3 on v2

v3 whole, which is shorter than its diff:
```python
import functools
import math

import jax
import jax.numpy as jnp
import numpy as np
from jax import lax
from jax.experimental import pallas as pl
from jax.experimental.pallas import tpu as pltpu
from jax.sharding import PartitionSpec as P

NLAT = 368
NLON = 1024
M = 512
SMAX = 24
LAT = 16
LON = 32
ROWS = 23
PAD = 24
COLS = 32
HALF = 128
X = LAT * PAD
MESH = pl.DeviceIdType.MESH


def split_pair(table):
    upper_part = table.astype(jnp.bfloat16)
    lower_part = (table - upper_part.astype(jnp.float32)).astype(jnp.bfloat16)
    return upper_part, lower_part


def doubled(table):
    upper = table.astype(jnp.bfloat16)
    lower = (table - upper.astype(np.float32)).astype(jnp.bfloat16)
    return np.concatenate([upper, lower], axis=-1)


def orders_of(bin_index, lat_index):
    first = bin_index + 32 * lat_index
    second = (496 if bin_index == 0 else 512) - first
    return first, second


@functools.lru_cache
def longitude_tables():
    turn = 2.0 * np.pi / NLON
    b = np.arange(32)
    step_one = np.zeros((2, 16, 32))
    for q in range(16):
        step_one[0, q] = np.cos(2 * np.pi * b * q / 32)
        step_one[1, q] = np.sin(2 * np.pi * b * q / 32) if q else (-1.0) ** b
    step_one = step_one.reshape(32, 32)
    r = np.arange(32)
    step_two = np.zeros((16, 2, 2, 16, 2, 32))
    weight = np.zeros((16, 2, 2, 16))
    for q in range(16):
        for a in range(16):
            for u, m in enumerate(orders_of(q, a)):
                cos, sin = np.cos(turn * ((m * r) % NLON)), np.sin(turn * ((m * r) % NLON))
                weight[q, u, :, a] = 1.0 if m == 0 else 2.0
                if q == 0:
                    step_two[q, u, 0, a, u] = cos
                    step_two[q, u, 1, a, u] = sin
                else:
                    sign = 1.0 if u == 0 else -1.0
                    step_two[q, u, 0, a, 0] = cos
                    step_two[q, u, 0, a, 1] = -sign * sin
                    step_two[q, u, 1, a, 0] = sin
                    step_two[q, u, 1, a, 1] = sign * cos
    step_two = step_two.reshape(16, 2, 2, 8, 2, 64).transpose(0, 2, 4, 1, 3, 5).reshape(16, 64, 64)
    weight = weight.reshape(16, 2, 2, 8, 2).transpose(0, 2, 4, 1, 3).reshape(16, 64, 1)
    back = np.swapaxes(step_two * weight, 1, 2)
    f32 = np.float32
    return (
        doubled(step_one.astype(f32)),
        doubled((step_two / NLON).astype(f32)),
        doubled(back.astype(f32)),
        doubled(step_one.T.astype(f32)),
    )


@functools.lru_cache
def cycle_tables():
    t = np.pi * (np.arange(NLAT) + 0.5) / NLAT
    f32 = np.float32

    def placed(values):
        padded = np.zeros((LAT, PAD))
        padded[:, :ROWS] = values.reshape(LAT, ROWS)
        return padded.reshape(4, 2, 2, 3, 8).transpose(3, 0, 2, 1, 4).astype(f32)

    weight = placed(np.sin(t) * np.pi / NLAT).reshape(3, 8, 2, 8).transpose(1, 0, 3, 2)
    weight = np.repeat(weight.reshape(8, PAD, 2), 64, axis=2)
    k = np.arange(1, M)
    log_norm = np.concatenate([[0.0], np.cumsum(np.log((2 * k - 1) / (2 * k)))])
    log_norm = 0.5 * np.log((2 * np.arange(M) + 1) / 2) + 0.5 * log_norm
    rows = np.stack(
        [placed(np.cos(t)).reshape(X), placed(np.log(np.sin(t))).reshape(X), placed(np.ones(NLAT)).reshape(X)]
    )
    return rows, weight, log_norm.reshape(1, M).astype(f32)


def dot(left, right):
    return jnp.dot(left, right, preferred_element_type=jnp.float32)


def twice(block):
    return jnp.concatenate([block, block], axis=0)


def trade(first, second):
    low = lax.broadcasted_iota(jnp.int32, first.shape, 1) < 64
    return (
        jnp.where(low, first, pltpu.roll(second, 64, axis=1)),
        jnp.where(low, pltpu.roll(first, 64, axis=1), second),
    )


def legendre_orders(bin_index, owner, cycle_rows, log_norm, up_table, down_table, table, legendre):
    f32 = jnp.float32

    def order_rows(slot):
        first = bin_index + 64 * owner + 32 * (slot // 2)
        return jnp.where(slot % 2 == 0, first, jnp.where(bin_index == 0, 496, 512) - first)

    def coefficients(block, _):
        row = lax.broadcasted_iota(jnp.int32, (128, HALF), 0)
        degree = (block * 32 + row // 4).astype(f32)
        order = order_rows(row % 4).astype(f32)
        gap, total = degree - order, degree + order
        inside = gap > 0.5
        odd = 2.0 * degree + 1.0
        shared = odd / jnp.where(inside, gap * total, 1.0)
        rise = jnp.sqrt(shared * jnp.maximum(2.0 * degree - 1.0, 0.0))
        fall = jnp.sqrt(
            shared * jnp.maximum((gap - 1.0) * (total - 1.0), 0.0) / jnp.maximum(2.0 * degree - 3.0, 1.0)
        )
        start = pl.multiple_of(block * 128, 128)
        up_table[pl.ds(start, 128), :] = jnp.where(inside, rise, 0.0)
        down_table[pl.ds(start, 128), :] = jnp.where(inside, fall, 0.0)
        return 0

    lax.fori_loop(0, 16, coefficients, 0)
    order = order_rows(lax.broadcasted_iota(jnp.int32, (4, X), 0))
    wide_order = order_rows(lax.broadcasted_iota(jnp.int32, (4, M), 0))
    column = lax.broadcasted_iota(jnp.int32, (4, M), 1)
    norm = jnp.sum(jnp.where(column == wide_order, log_norm[...], 0.0), axis=1, keepdims=True)
    cosines = jnp.broadcast_to(cycle_rows[pl.ds(0, 1), :], (4, X))
    log_start = norm + order.astype(f32) * cycle_rows[pl.ds(1, 1), :]
    start_scale = jnp.minimum(log_start, 0.0)
    diagonal = jnp.exp(log_start - start_scale) * cycle_rows[pl.ds(2, 1), :]

    def spread(rows):
        return jnp.concatenate([rows] * (X // HALF), axis=1)

    def steps(block, state):
        latest, before, log_scale = state
        factor = jnp.exp(log_scale)
        for k in range(4):
            degree = block * 4 + k
            up = spread(up_table[pl.ds(4 * degree, 4), :]) * cosines
            down = spread(down_table[pl.ds(4 * degree, 4), :])
            current = up * latest + (jnp.where(order == degree, diagonal, 0.0) - down * before)
            value = current * factor
            for lane in range(X // HALF):
                table[lane, pl.ds(4 * degree, 4), :] = value[:, lane * HALF : (lane + 1) * HALF]
            latest, before = current, latest
        too_big = jnp.abs(latest) > 2.0**24
        shrink = jnp.where(too_big, 2.0**-24, 1.0)
        log_scale = jnp.where(too_big, log_scale + 24.0 * math.log(2.0), log_scale)
        return latest * shrink, before * shrink, log_scale

    blank = jnp.zeros((4, X), f32)
    lax.fori_loop(0, M // 4, steps, (blank, blank, start_scale))
    for slot in range(4):
        for lane in range(X // HALF):
            legendre[slot, :, lane * HALF : (lane + 1) * HALF] = table[
                lane, pl.ds(slot, M, stride=4), :
            ].astype(jnp.bfloat16)


def block_kernel(
    fields_in, conv_in, gain_in, support_in, one_in, two_in, three_in, four_in, cycles_in,
    weight_in, norm_in,
    out,
    s1, g1, s2, g2, s3, g3, s4, g4, s5, g5, s6, g6, wide, edge_out, edge_in, pooled, convolved,
    near, far, plain,
    up_table, down_table, table, legendre, gains, total,
    cycles, conv_weight, gain, support, one, two, three, four, cycle_rows, weight, log_norm,
    fetch, send, recv, halo_send, halo_recv, ready,
):
    lat = lax.axis_index("lat")
    lon = lax.axis_index("lon")
    hemi = lat // 2 % 2
    owner = lat // 4 * 2 + lat % 2
    spot = hemi * LON + lon
    bin_index, half_index = lon // 2, lon % 2
    f32, bf16 = jnp.float32, jnp.bfloat16

    def double_peer(step):
        index = (spot + step) % (2 * LON)
        return index, (lat // 4 * 4 + index // LON * 2 + lat % 2, index % LON)

    def owner_peer(step):
        index = (owner + step) % 8
        return index, (index // 2 * 4 + hemi * 2 + index % 2, lon)

    def ring_peer(step):
        index = (lon + step) % LON
        return index, (lat, index)

    barrier = pltpu.get_barrier_semaphore()

    def greet(peer_of):
        def one_peer(step, _):
            pl.semaphore_signal(barrier, inc=1, device_id=peer_of(step)[1], device_id_type=MESH)
            return 0

        return one_peer

    partner = (lat // 4 * 4 + (1 - hemi) * 2 + lat % 2, lon)
    lax.fori_loop(1, LON, greet(ring_peer), 0)
    lax.fori_loop(1, 8, greet(owner_peer), 0)
    for device in (((lat + 1) % LAT, lon), ((lat + LAT - 1) % LAT, lon), partner):
        pl.semaphore_signal(barrier, inc=1, device_id=device, device_id_type=MESH)

    own_lanes = pl.ds(pl.multiple_of(half_index * HALF, HALF), HALF)
    sources = [
        (fields_in, cycles.at[pl.ds(1, ROWS)]), (cycles_in, cycle_rows), (norm_in, log_norm), (one_in, one),
        (gain_in.at[:, own_lanes], gain), (two_in.at[bin_index], two),
        (weight_in.at[owner], weight), (three_in.at[bin_index], three), (support_in, support),
        (four_in, four), (conv_in, conv_weight),
    ]
    fetches = [
        pltpu.make_async_copy(source, target, fetch.at[index])
        for index, (source, target) in enumerate(sources)
    ]
    for copy in fetches:
        copy.start()

    ring = (ring_peer, lon, LON)
    double = (double_peer, spot, 2 * LON)
    owners = (owner_peer, owner, 8)
    plan = [
        (s1, g1, ring), (s2, g2, double), (s3, g3, owners),
        (s4, g4, owners), (s5, g5, double), (s6, g6, ring),
    ]

    def exchange(stage, chunk):
        source, target, (peer_of, mine, count) = plan[stage]

        def one_peer(step, _):
            peer, device = peer_of(step)
            pltpu.make_async_remote_copy(
                src_ref=source.at[chunk, peer], dst_ref=target.at[chunk, mine],
                send_sem=send.at[stage, chunk], recv_sem=recv.at[stage, chunk],
                device_id=device, device_id_type=MESH,
            ).start()
            return 0

        lax.fori_loop(1, count, one_peer, 0)
        target[chunk, mine] = source[chunk, mine]

    def whole(stage, chunk):
        source, target, (_, _, count) = plan[stage]
        return pltpu.make_async_remote_copy(
            src_ref=source.at[chunk, pl.ds(0, count - 1)],
            dst_ref=target.at[chunk, pl.ds(0, count - 1)],
            send_sem=send.at[stage, chunk], recv_sem=recv.at[stage, chunk],
            device_id=(lat, (lon + 1) % LON), device_id_type=MESH,
        )

    def arrived(stage, chunk):
        whole(stage, chunk).wait_recv()
        target = plan[stage][1]
        return target[chunk].astype(f32).reshape(512, HALF)

    fetches[0].wait()
    for half in range(2):
        lanes = slice(half * HALF, (half + 1) * HALF)
        plain[half, pl.ds(0, ROWS * COLS), :] = (
            cycles[1 : ROWS + 1, :, lanes].astype(f32).reshape(ROWS * COLS, HALF)
        )
        plain[half, pl.ds(ROWS * COLS, COLS), :] = jnp.zeros((COLS, HALF), f32)

    for chunk in range(3):

        def pack_residue(r, _, chunk=chunk):
            rows = [
                plain[half, pl.ds(chunk * 8 * COLS + r, 8, stride=COLS), :] for half in range(2)
            ]
            s1[chunk, r] = jnp.concatenate(rows, axis=0).astype(bf16)
            return 0

        lax.fori_loop(0, LON, pack_residue, 0)
        if chunk == 0:
            pl.semaphore_wait(barrier, LON - 1 + 7 + 3)
            pl.semaphore_signal(ready, inc=1, device_id=partner, device_id_type=MESH)
        exchange(0, chunk)

    halo_down = pltpu.make_async_remote_copy(
        src_ref=cycles.at[ROWS], dst_ref=cycles.at[0], send_sem=halo_send.at[2],
        recv_sem=halo_recv.at[2], device_id=((lat + 1) % LAT, lon), device_id_type=MESH,
    )
    halo_up = pltpu.make_async_remote_copy(
        src_ref=cycles.at[1], dst_ref=cycles.at[ROWS + 1], send_sem=halo_send.at[3],
        recv_sem=halo_recv.at[3], device_id=((lat + LAT - 1) % LAT, lon), device_id_type=MESH,
    )
    halo_down.start()
    halo_up.start()

    for copy in fetches[1:]:
        copy.wait()
    legendre_orders(
        bin_index, owner, cycle_rows, log_norm, up_table, down_table, table, legendre
    )
    turned = pltpu.roll(gain[...], 64, axis=1)
    lane_half = lax.broadcasted_iota(jnp.int32, (M, HALF), 1) // 64
    gains[...] = jnp.where(lane_half == hemi, gain[...], turned)

    for chunk in range(3):
        far[...] = arrived(0, chunk)
        block = jnp.concatenate(
            [far[pl.ds(n, 32, stride=16), :] for n in range(16)], axis=1
        ).astype(bf16)
        result = dot(one[...], twice(block))
        for n in range(16):
            half, row = divmod(n, 8)
            lanes = slice(n * HALF, (n + 1) * HALF)
            quarters = trade(result[0:16, lanes], result[16:32, lanes])
            for g in range(2):
                near[pl.ds((g * LON + half) * 8 + row, 16, stride=16), :] = quarters[g]
        s2[chunk] = near[...].reshape(2 * LON, 8, HALF).astype(bf16)
        if chunk == 0:
            pl.semaphore_wait(ready, 1)
        exchange(1, chunk)

    halo_down.wait_recv()
    halo_up.wait_recv()
    edge = jnp.full((COLS, 2 * HALF), lat, jnp.int32)
    cycles[0] = jnp.where(edge > 0, cycles[0].astype(f32), 0.0).astype(bf16)
    cycles[ROWS + 1] = jnp.where(edge < LAT - 1, cycles[ROWS + 1].astype(f32), 0.0).astype(bf16)

    def pack_edges(y, _):
        row = cycles[y].astype(f32)
        edge_out[0, y] = row[COLS - SMAX :].astype(bf16)
        edge_out[1, y] = row[:SMAX].astype(bf16)
        return 0

    lax.fori_loop(0, ROWS + 2, pack_edges, 0)
    halo_right = pltpu.make_async_remote_copy(
        src_ref=edge_out.at[0], dst_ref=edge_in.at[0],
        send_sem=halo_send.at[0], recv_sem=halo_recv.at[0],
        device_id=(lat, (lon + 1) % LON), device_id_type=MESH,
    )
    halo_left = pltpu.make_async_remote_copy(
        src_ref=edge_out.at[1], dst_ref=edge_in.at[1],
        send_sem=halo_send.at[1], recv_sem=halo_recv.at[1],
        device_id=(lat, (lon + LON - 1) % LON), device_id_type=MESH,
    )

    for chunk in range(3):
        far[...] = arrived(1, chunk)
        if chunk == 2:
            halo_right.start()
            halo_left.start()
        columns = [
            jnp.concatenate(
                trade(far[pl.ds(row, 32, stride=8), :], far[pl.ds(256 + row, 32, stride=8), :]),
                axis=0,
            )
            for row in range(8)
        ]
        result = dot(two[...], twice(jnp.concatenate(columns, axis=1).astype(bf16)))
        for row in range(8):
            scaled = result[:, row * HALF : (row + 1) * HALF] * weight[pl.ds(chunk * 8 + row, 1), :]
            sides = trade(scaled[0:32], scaled[32:64])
            for g in range(2):
                for slot in range(4):
                    near[pl.ds(slot * 16 + g * 8 + row, 8, stride=64), :] = sides[g][
                        slot * 8 : slot * 8 + 8
                    ]
        s3[chunk] = near[...].reshape(8, 64, HALF).astype(bf16)
        exchange(2, chunk)

    for chunk in range(3):
        whole(2, chunk).wait_recv()
        lanes = slice(chunk * HALF, (chunk + 1) * HALF)
        for slot in range(4):
            data = g3[chunk, :, slot * 16 : slot * 16 + 16, :].reshape(HALF, HALF)
            part = dot(legendre[slot, :, lanes], data)
            if chunk == 0:
                total[slot] = part
            elif chunk == 1:
                total[slot] += part
            else:
                pooled[pl.ds(0, M), pl.ds(slot * HALF, HALF)] = (
                    (total[slot] + part) * gains[...]
                ).astype(bf16)
    for chunk in range(3):
        lanes = slice(chunk * HALF, (chunk + 1) * HALF)
        for slot in range(4):
            synthesis = lax.dot_general(
                legendre[slot, :, lanes],
                pooled[pl.ds(0, M), pl.ds(slot * HALF, HALF)],
                (((0,), (0,)), ((), ())),
                preferred_element_type=f32,
            )
            s4[chunk, :, slot * 16 : slot * 16 + 16, :] = synthesis.reshape(8, 16, HALF).astype(bf16)
        exchange(3, chunk)

    for chunk in range(3):
        far[...] = arrived(3, chunk)
        columns = []
        for row in range(8):
            sides = [
                jnp.concatenate(
                    [far[pl.ds(slot * 16 + g * 8 + row, 8, stride=64), :] for slot in range(4)],
                    axis=0,
                )
                for g in range(2)
            ]
            columns.append(jnp.concatenate(trade(*sides), axis=0))
        result = dot(three[...], twice(jnp.concatenate(columns, axis=1).astype(bf16)))
        for row in range(8):
            lanes = slice(row * HALF, (row + 1) * HALF)
            sides = trade(result[0:32, lanes], result[32:64, lanes])
            for g in range(2):
                near[pl.ds(g * 256 + row, 32, stride=8), :] = sides[g]
        s5[chunk] = near[...].reshape(2 * LON, 8, HALF).astype(bf16)
        exchange(4, chunk)

    halo_right.wait_recv()
    halo_left.wait_recv()

    def widen(y, _):
        sides = [edge_in[0, y], cycles[y], edge_in[1, y]]
        wide[y] = jnp.concatenate([side.astype(f32) for side in sides], axis=0).astype(bf16)
        return 0

    lax.fori_loop(0, ROWS + 2, widen, 0)
    source = lax.broadcasted_iota(jnp.int32, (COLS, COLS + 2 * SMAX), 1)
    target = lax.broadcasted_iota(jnp.int32, (COLS, COLS + 2 * SMAX), 0)
    offset = source - target - SMAX
    offset_real = offset.astype(f32)
    distance = jnp.abs(offset)
    distance_real = distance.astype(f32)

    def pool(y, _):
        half_width = jnp.full((COLS, COLS + 2 * SMAX), support[y], jnp.int32)
        span_len = (half_width + 1).astype(f32)
        inside = distance <= half_width
        triangle = jnp.where(inside, (span_len - distance_real) / span_len, 0.0)
        odd_basis = offset_real * triangle / span_len
        box_basis = jnp.where(inside, 1.0, 0.0) / jnp.sqrt(2.0 * half_width.astype(f32) + 1.0)
        band = jnp.concatenate([triangle, odd_basis, box_basis], axis=0).astype(bf16)
        start = pl.multiple_of(y * COLS, COLS)
        for a in range(3):
            basis = dot(band, wide[y + a]).astype(bf16)
            for k in range(3):
                pooled[pl.ds(start, COLS), pl.ds((a * 3 + k) * 256, 256)] = basis[
                    k * COLS : (k + 1) * COLS
                ]
        return 0

    lax.fori_loop(0, ROWS, pool, 0)

    for chunk in range(3):
        far[...] = arrived(4, chunk)
        columns = [
            jnp.concatenate(
                trade(far[pl.ds(n, 16, stride=16), :], far[pl.ds(256 + n, 16, stride=16), :]), axis=0
            )
            for n in range(16)
        ]
        result = dot(four[...], twice(jnp.concatenate(columns, axis=1).astype(bf16)))
        for n in range(16):
            near[pl.ds(n, 32, stride=16), :] = result[:, n * HALF : (n + 1) * HALF]
        s6[chunk] = near[...].reshape(LON, 16, HALF).astype(bf16)
        exchange(5, chunk)

    rows = ROWS * COLS // 4
    for part in range(4):
        convolved[part * rows : (part + 1) * rows, :] = dot(
            pooled[part * rows : (part + 1) * rows, :], conv_weight[...]
        )

    for chunk in range(3):
        far[...] = arrived(5, chunk)
        for row in range(8 if chunk < 2 else 7):
            y = chunk * 8 + row
            spectral = jnp.concatenate(
                [far[pl.ds(half * 8 + row, 32, stride=16), :] for half in range(2)], axis=1
            )
            branch = convolved[pl.ds(y * COLS, COLS), :] + spectral
            gelu = 0.5 * branch * (1.0 + lax.erf(branch * math.sqrt(0.5)))
            out[y] = (cycles[y + 1].astype(f32) + gelu).astype(bf16)

    for stage in range(6):
        for chunk in range(3):
            whole(stage, chunk).wait_send()
    for copy in (halo_right, halo_left, halo_down, halo_up):
        copy.wait_send()


def per_device(fields, conv_weight, spectral_gain, support):
    vmem = pl.BlockSpec(memory_space=pltpu.VMEM)
    hbm = pl.BlockSpec(memory_space=pltpu.HBM)
    f32, bf16 = jnp.float32, jnp.bfloat16
    by_ring = pltpu.VMEM((3, LON, 16, HALF), bf16)
    by_double = pltpu.VMEM((3, 2 * LON, 8, HALF), bf16)
    by_owner = pltpu.VMEM((3, 8, 64, HALF), bf16)
    tables = longitude_tables() + cycle_tables()
    return pl.pallas_call(
        block_kernel,
        out_shape=jax.ShapeDtypeStruct(fields.shape, fields.dtype),
        in_specs=[hbm] * 11,
        out_specs=vmem,
        scratch_shapes=[by_ring] * 2
        + [by_double] * 2
        + [by_owner] * 4
        + [by_double] * 2
        + [by_ring] * 2
        + [
            pltpu.VMEM((ROWS + 2, COLS + 2 * SMAX, 256), bf16),
            pltpu.VMEM((2, ROWS + 2, SMAX, 256), bf16),
            pltpu.VMEM((2, ROWS + 2, SMAX, 256), bf16),
            pltpu.VMEM((ROWS * COLS, 9 * 256), bf16),
            pltpu.VMEM((ROWS * COLS, 256), f32),
            pltpu.VMEM((512, HALF), f32),
            pltpu.VMEM((512, HALF), f32),
            pltpu.VMEM((2, PAD * COLS, HALF), f32),
            pltpu.VMEM((4 * M, HALF), f32),
            pltpu.VMEM((4 * M, HALF), f32),
            pltpu.VMEM((X // HALF, 4 * M, HALF), f32),
            pltpu.VMEM((4, M, X), bf16),
            pltpu.VMEM((M, HALF), f32),
            pltpu.VMEM((4, M, HALF), f32),
            pltpu.VMEM((ROWS + 2, COLS, 256), bf16),
            pltpu.VMEM((9 * 256, 256), bf16),
            pltpu.VMEM((M, HALF), f32),
            pltpu.SMEM((ROWS,), jnp.int32),
            pltpu.VMEM((32, 64), bf16),
            pltpu.VMEM((64, 128), bf16),
            pltpu.VMEM((64, 128), bf16),
            pltpu.VMEM((32, 64), bf16),
            pltpu.VMEM((3, X), f32),
            pltpu.VMEM((PAD, HALF), f32),
            pltpu.VMEM((1, M), f32),
            pltpu.SemaphoreType.DMA((11,)),
            pltpu.SemaphoreType.DMA((6, 3)),
            pltpu.SemaphoreType.DMA((6, 3)),
            pltpu.SemaphoreType.DMA((4,)),
            pltpu.SemaphoreType.DMA((4,)),
            pltpu.SemaphoreType.REGULAR,
        ],
        compiler_params=pltpu.CompilerParams(
            collective_id=0, has_side_effects=True, vmem_limit_bytes=48 * 2**20
        ),
    )(
        fields, conv_weight.reshape(9 * 256, 256), spectral_gain, support,
        *[jnp.asarray(table) for table in tables],
    )


def solution(mesh):
    placed = (P("lat", "lon", None), P(), P(), P("lat"))
    return jax.shard_map(
        per_device, mesh=mesh, in_specs=placed, out_specs=P("lat", "lon", None), check_vma=False
    )
```

time: 96.9 us -> 84 us (0.87)
  Pallas kernels: 85.5 us -> 73.2 us
    pallas_call x1, Pallas kernels: 85.5 us -> 73.2 us  [per_device(): pl.pallas_call(block_kernel, out_shape=jax.ShapeDtypeStruct(fields.shape,...]
where the time goes in v3:
time: 84 us; the launch traced here: 83.5 us
  Pallas kernels  73.2 us (87%)
  local copies, waits for them, and re-layouts  10.3 us (12%)
    pallas_call x1, Pallas kernels, per_device(): pl.pallas_call(block_kernel, out_shape=jax.ShapeDtypeStruct(fields.shape,...  73.2 us
    unnamed x23, local copies, waits for them, and re-layouts  10.3 us

profile of v3, /device:TPU:1, one launch (start us, length us, event | category | flops | bytes accessed | tf_op | source)
XLA Modules:
  0.0 83.5 jit_solution(13386202149428573343)
XLA Ops:
  0.0 0.0 copy-start
  0.0 1.3 %copy-done = bf16[3,3,256,256]{3,2,1,0:T(8,128)(2,1)S(1)} copy-done((bf16[3,3,256,256]{3,2,1,0:T(8,128)(2,1)S(1)}, bf16[3,3,256,256]{3,2,1,0:T(8,128)(2,1)}, u32[]{:S(2)}) %copy-start) | copy-done | bytes 1179672
  1.3 0.0 copy-start.1
  1.3 1.0 %copy-done.1 = f32[512,256]{1,0:T(8,128)S(1)} copy-done((f32[512,256]{1,0:T(8,128)S(1)}, f32[512,256]{1,0:T(8,128)}, u32[]{:S(2)}) %copy-start.1) | copy-done | bytes 524312
  2.3 0.0 copy-start.2
  2.3 1.0 %copy-done.2 = bf16[23,32,256]{2,1,0:T(8,128)(2,1)S(1)} copy-done((bf16[23,32,256]{2,1,0:T(8,128)(2,1)S(1)}, bf16[23,32,256]{2,1,0:T(8,128)(2,1)}, u32[]{:S(2)}) %copy-start.2) | copy-done | bytes 376856
  3.3 0.0 copy-start.3
  3.3 0.9 %copy-done.3 = bf16[16,64,128]{2,1,0:T(8,128)(2,1)S(1)} copy-done((bf16[16,64,128]{2,1,0:T(8,128)(2,1)S(1)}, bf16[16,64,128]{2,1,0:T(8,128)(2,1)}, u32[]{:S(2)}) %copy-start.3) | copy-done | bytes 262168
  4.3 0.0 copy-start.4
  4.3 0.9 %copy-done.4 = bf16[16,64,128]{2,1,0:T(8,128)(2,1)S(1)} copy-done((bf16[16,64,128]{2,1,0:T(8,128)(2,1)S(1)}, bf16[16,64,128]{2,1,0:T(8,128)(2,1)}, u32[]{:S(2)}) %copy-start.4) | copy-done | bytes 262168
  5.2 0.0 copy-start.5
  5.2 0.9 %copy-done.5 = f32[8,24,128]{2,1,0:T(8,128)S(1)} copy-done((f32[8,24,128]{2,1,0:T(8,128)S(1)}, f32[8,24,128]{2,1,0:T(8,128)}, u32[]{:S(2)}) %copy-start.5) | copy-done | bytes 98328
  6.1 0.0 copy-start.6
  6.1 0.7 copy-done.6
  6.8 0.0 copy-start.7
  6.8 0.7 copy-done.7
  7.5 0.0 copy-start.8
  7.5 0.7 copy-done.8
  8.2 0.0 copy-start.9
  8.2 0.7 copy-done.9
  8.9 0.0 copy-start.10
  8.9 0.7 copy-done.10
  9.5 73.2 %shard_map.109 = bf16[23,32,256]{2,1,0:T(8,128)(2,1)S(1)} custom-call(bf16[23,32,256]{2,1,0:T(8,128)(2,1)S(1)} %copy-done.2, bf16[2304,256]{1,0:T(8,128)(2,1)S(1)} %bitcast.1, f32[512,256]{1,0:T(8,128)S(1)} %copy-done.1, s32[23]{0:T(128)S(1)} %copy-done.10, bf16[32,64]{1,0:T(8,128)(2,1)S(1)} %copy-done.7, bf16[16,64,128]{2,1,0:T(8,128)(2,1)S(1)} %copy-done.4, ...), custom_call_target="tpu_custom_call" | custom-call | tf_op jit(solution)/shard_map/pallas_call | solution.py:514
  82.7 0.7 copy.13
Async XLA Ops:
  0.0 1.3 %copy-start = (bf16[3,3,256,256]{3,2,1,0:T(8,128)(2,1)S(1)}, bf16[3,3,256,256]{3,2,1,0:T(8,128)(2,1)}, u32[]{:S(2)}) copy-start(bf16[3,3,256,256]{3,2,1,0:T(8,128)(2,1)} %param.12) | copy-start | bytes 3538948
  1.3 1.0 %copy-start.1 = (f32[512,256]{1,0:T(8,128)S(1)}, f32[512,256]{1,0:T(8,128)}, u32[]{:S(2)}) copy-start(f32[512,256]{1,0:T(8,128)} %gain_in.1) | copy-start | bytes 1572868
  2.3 1.0 %copy-start.2 = (bf16[23,32,256]{2,1,0:T(8,128)(2,1)S(1)}, bf16[23,32,256]{2,1,0:T(8,128)(2,1)}, u32[]{:S(2)}) copy-start(bf16[23,32,256]{2,1,0:T(8,128)(2,1)} %fields_in.1) | copy-start | bytes 1130500
  3.3 0.9 %copy-start.3 = (bf16[16,64,128]{2,1,0:T(8,128)(2,1)S(1)}, bf16[16,64,128]{2,1,0:T(8,128)(2,1)}, u32[]{:S(2)}) copy-start(bf16[16,64,128]{2,1,0:T(8,128)(2,1)} %constant.16.clone.three_in) | copy-start | bytes 786436
  4.3 0.9 %copy-start.4 = (bf16[16,64,128]{2,1,0:T(8,128)(2,1)S(1)}, bf16[16,64,128]{2,1,0:T(8,128)(2,1)}, u32[]{:S(2)}) copy-start(bf16[16,64,128]{2,1,0:T(8,128)(2,1)} %constant.15.clone.two_in) | copy-start | bytes 786436
  5.2 0.9 %copy-start.5 = (f32[8,24,128]{2,1,0:T(8,128)S(1)}, f32[8,24,128]{2,1,0:T(8,128)}, u32[]{:S(2)}) copy-start(f32[8,24,128]{2,1,0:T(8,128)} %constant.19.clone.weight_in) | copy-start | bytes 294916
  6.1 0.7 copy-start.6
  6.8 0.7 copy-start.7
  7.5 0.7 copy-start.8
  8.2 0.7 copy-start.9
  8.9 0.7 copy-start.10

commit v4 on v3

--- a/solution.py
+++ b/solution.py
@@ -555,7 +555,7 @@
             pltpu.SemaphoreType.REGULAR,
         ],
         compiler_params=pltpu.CompilerParams(
-            collective_id=0, has_side_effects=True, vmem_limit_bytes=48 * 2**20
+            collective_id=0, has_side_effects=True, vmem_limit_bytes=64 * 2**20
         ),
     )(
         fields, conv_weight.reshape(9 * 256, 256), spectral_gain, support,

time: 84 us -> 75.9 us (0.904)
  local copies, waits for them, and re-layouts: 10.3 us -> 1.76 us
    unnamed x23 -> x1, local copies, waits for them, and re-layouts: 10.3 us -> 1.76 us
where the time goes in v4:
time: 75.9 us; the launch traced here: 75.7 us
  Pallas kernels  73.9 us (97%)
  local copies, waits for them, and re-layouts  1.76 us (2%)
    pallas_call x1, Pallas kernels, per_device(): pl.pallas_call(block_kernel, out_shape=jax.ShapeDtypeStruct(fields.shape,...  73.9 us
    unnamed x1, local copies, waits for them, and re-layouts  1.76 us

profile of v4, /device:TPU:1, one launch (start us, length us, event | category | flops | bytes accessed | tf_op | source)
XLA Modules:
  0.0 75.7 jit_solution(7501722611885908319)
XLA Ops:
  0.0 73.9 %shard_map.109 = bf16[23,32,256]{2,1,0:T(8,128)(2,1)} custom-call(bf16[23,32,256]{2,1,0:T(8,128)(2,1)} %fields_in.1, bf16[2304,256]{1,0:T(8,128)(2,1)} %bitcast.1, f32[512,256]{1,0:T(8,128)} %gain_in.1, s32[23]{0:T(128)} %support_in.1, bf16[32,64]{1,0:T(8,128)(2,1)} %constant.14.clone.one_in, bf16[16,64,128]{2,1,0:T(8,128)(2,1)} %constant.15.clone.two_in, ...), custom_call_target="tpu_custom_call" | custom-call | tf_op jit(solution)/shard_map/pallas_call | solution.py:514
  73.9 1.8 %copy.13 = bf16[23,32,256]{2,1,0:T(8,128)(2,1)} copy(bf16[23,32,256]{2,1,0:T(8,128)(2,1)} %shard_map.109) | data formatting | bytes 753664

commit v5 on v4

--- a/solution.py
+++ b/solution.py
@@ -171,12 +171,15 @@
         return latest * shrink, before * shrink, log_scale
 
     blank = jnp.zeros((4, X), f32)
-    lax.fori_loop(0, M // 4, steps, (blank, blank, start_scale))
+    state = lax.fori_loop(0, M // 8, steps, (blank, blank, start_scale))
+    yield
+    lax.fori_loop(M // 8, M // 4, steps, state)
     for slot in range(4):
         for lane in range(X // HALF):
             legendre[slot, :, lane * HALF : (lane + 1) * HALF] = table[
                 lane, pl.ds(slot, M, stride=4), :
             ].astype(jnp.bfloat16)
+    yield
 
 
 def block_kernel(
@@ -194,35 +197,9 @@
     hemi = lat // 2 % 2
     owner = lat // 4 * 2 + lat % 2
     spot = hemi * LON + lon
+    double_base = lat // 4 * 4 + lat % 2
     bin_index, half_index = lon // 2, lon % 2
     f32, bf16 = jnp.float32, jnp.bfloat16
-
-    def double_peer(step):
-        index = (spot + step) % (2 * LON)
-        return index, (lat // 4 * 4 + index // LON * 2 + lat % 2, index % LON)
-
-    def owner_peer(step):
-        index = (owner + step) % 8
-        return index, (index // 2 * 4 + hemi * 2 + index % 2, lon)
-
-    def ring_peer(step):
-        index = (lon + step) % LON
-        return index, (lat, index)
-
-    barrier = pltpu.get_barrier_semaphore()
-
-    def greet(peer_of):
-        def one_peer(step, _):
-            pl.semaphore_signal(barrier, inc=1, device_id=peer_of(step)[1], device_id_type=MESH)
-            return 0
-
-        return one_peer
-
-    partner = (lat // 4 * 4 + (1 - hemi) * 2 + lat % 2, lon)
-    lax.fori_loop(1, LON, greet(ring_peer), 0)
-    lax.fori_loop(1, 8, greet(owner_peer), 0)
-    for device in (((lat + 1) % LAT, lon), ((lat + LAT - 1) % LAT, lon), partner):
-        pl.semaphore_signal(barrier, inc=1, device_id=device, device_id_type=MESH)
 
     own_lanes = pl.ds(pl.multiple_of(half_index * HALF, HALF), HALF)
     sources = [
@@ -235,7 +212,35 @@
         pltpu.make_async_copy(source, target, fetch.at[index])
         for index, (source, target) in enumerate(sources)
     ]
-    for copy in fetches:
+    fetches[0].start()
+
+    def double_peer(step):
+        index = lax.rem(spot + step, 2 * LON)
+        return index, (double_base + lax.div(index, LON) * 2, lax.rem(index, LON))
+
+    def owner_peer(step):
+        index = lax.rem(owner + step, 8)
+        return index, (lax.div(index, 2) * 4 + hemi * 2 + lax.rem(index, 2), lon)
+
+    def ring_peer(step):
+        index = lax.rem(lon + step, LON)
+        return index, (lat, index)
+
+    barrier = pltpu.get_barrier_semaphore()
+
+    def greet(peer_of):
+        def one_peer(step, _):
+            pl.semaphore_signal(barrier, inc=1, device_id=peer_of(step)[1], device_id_type=MESH)
+            return 0
+
+        return one_peer
+
+    partner = (lat // 4 * 4 + (1 - hemi) * 2 + lat % 2, lon)
+    lax.fori_loop(1, LON, greet(ring_peer), 0)
+    lax.fori_loop(1, 8, greet(owner_peer), 0)
+    for device in (((lat + 1) % LAT, lon), ((lat + LAT - 1) % LAT, lon), partner):
+        pl.semaphore_signal(barrier, inc=1, device_id=device, device_id_type=MESH)
+    for copy in fetches[1:]:
         copy.start()
 
     ring = (ring_peer, lon, LON)
@@ -276,14 +281,17 @@
         return target[chunk].astype(f32).reshape(512, HALF)
 
     fetches[0].wait()
-    for half in range(2):
-        lanes = slice(half * HALF, (half + 1) * HALF)
-        plain[half, pl.ds(0, ROWS * COLS), :] = (
-            cycles[1 : ROWS + 1, :, lanes].astype(f32).reshape(ROWS * COLS, HALF)
-        )
-        plain[half, pl.ds(ROWS * COLS, COLS), :] = jnp.zeros((COLS, HALF), f32)
-
-    for chunk in range(3):
+    for chunk in range(3):
+        count = min(8, ROWS - chunk * 8)
+        for half in range(2):
+            lanes = slice(half * HALF, (half + 1) * HALF)
+            plain[half, pl.ds(chunk * 8 * COLS, count * COLS), :] = (
+                cycles[chunk * 8 + 1 : chunk * 8 + 1 + count, :, lanes]
+                .astype(f32)
+                .reshape(count * COLS, HALF)
+            )
+            if count < 8:
+                plain[half, pl.ds(ROWS * COLS, COLS), :] = jnp.zeros((COLS, HALF), f32)
 
         def pack_residue(r, _, chunk=chunk):
             rows = [
@@ -311,9 +319,10 @@
 
     for copy in fetches[1:]:
         copy.wait()
-    legendre_orders(
+    making = legendre_orders(
         bin_index, owner, cycle_rows, log_norm, up_table, down_table, table, legendre
     )
+    next(making)
     turned = pltpu.roll(gain[...], 64, axis=1)
     lane_half = lax.broadcasted_iota(jnp.int32, (M, HALF), 1) // 64
     gains[...] = jnp.where(lane_half == hemi, gain[...], turned)
@@ -334,6 +343,8 @@
         if chunk == 0:
             pl.semaphore_wait(ready, 1)
         exchange(1, chunk)
+
+    next(making)
 
     halo_down.wait_recv()
     halo_up.wait_recv()

time: 75.9 us -> 74.8 us (0.986)
  Pallas kernels: 73.9 us -> 72.9 us
    pallas_call x1, Pallas kernels: 73.9 us -> 72.9 us  [per_device(): pl.pallas_call(block_kernel, out_shape=jax.ShapeDtypeStruct(fields.shape,...]
where the time goes in v5:
time: 74.8 us; the launch traced here: 74.6 us
  Pallas kernels  72.9 us (97%)
  local copies, waits for them, and re-layouts  1.76 us (2%)
    pallas_call x1, Pallas kernels, per_device(): pl.pallas_call(block_kernel, out_shape=jax.ShapeDtypeStruct(fields.shape,...  72.9 us
    unnamed x1, local copies, waits for them, and re-layouts  1.76 us

profile of v5, /device:TPU:1, one launch (start us, length us, event | category | flops | bytes accessed | tf_op | source)
XLA Modules:
  0.0 74.6 jit_solution(7306703759465807140)
XLA Ops:
  0.0 72.9 %shard_map.109 = bf16[23,32,256]{2,1,0:T(8,128)(2,1)} custom-call(bf16[23,32,256]{2,1,0:T(8,128)(2,1)} %fields_in.1, bf16[2304,256]{1,0:T(8,128)(2,1)} %bitcast.1, f32[512,256]{1,0:T(8,128)} %gain_in.1, s32[23]{0:T(128)} %support_in.1, bf16[32,64]{1,0:T(8,128)(2,1)} %constant.14.clone.one_in, bf16[16,64,128]{2,1,0:T(8,128)(2,1)} %constant.15.clone.two_in, ...), custom_call_target="tpu_custom_call" | custom-call | tf_op jit(solution)/shard_map/pallas_call | solution.py:525
  72.9 1.8 %copy.13 = bf16[23,32,256]{2,1,0:T(8,128)(2,1)} copy(bf16[23,32,256]{2,1,0:T(8,128)(2,1)} %shard_map.109) | data formatting | bytes 753664

commit v6 on v5

--- a/solution.py
+++ b/solution.py
@@ -254,16 +254,22 @@
     def exchange(stage, chunk):
         source, target, (peer_of, mine, count) = plan[stage]
 
-        def one_peer(step, _):
+        def one_peer(step):
             peer, device = peer_of(step)
             pltpu.make_async_remote_copy(
                 src_ref=source.at[chunk, peer], dst_ref=target.at[chunk, mine],
                 send_sem=send.at[stage, chunk], recv_sem=recv.at[stage, chunk],
                 device_id=device, device_id_type=MESH,
             ).start()
+
+        def three_peers(turn, _):
+            for k in range(3):
+                one_peer(turn * 3 + 1 + k)
             return 0
 
-        lax.fori_loop(1, count, one_peer, 0)
+        lax.fori_loop(0, (count - 1) // 3, three_peers, 0)
+        if (count - 1) % 3:
+            one_peer(count - 1)
         target[chunk, mine] = source[chunk, mine]
 
     def whole(stage, chunk):

time: 74.8 us -> 74.4 us (level)
  no operation moved by 1% of the time
where the time goes in v6:
time: 74.4 us; the launch traced here: 74.1 us
  Pallas kernels  72.4 us (97%)
  local copies, waits for them, and re-layouts  1.76 us (2%)
    pallas_call x1, Pallas kernels, per_device(): pl.pallas_call(block_kernel, out_shape=jax.ShapeDtypeStruct(fields.shape,...  72.4 us
    unnamed x1, local copies, waits for them, and re-layouts  1.76 us

profile of v6, /device:TPU:1, one launch (start us, length us, event | category | flops | bytes accessed | tf_op | source)
XLA Modules:
  0.0 74.1 jit_solution(10416048152103817125)
XLA Ops:
  0.0 72.4 %shard_map.109 = bf16[23,32,256]{2,1,0:T(8,128)(2,1)} custom-call(bf16[23,32,256]{2,1,0:T(8,128)(2,1)} %fields_in.1, bf16[2304,256]{1,0:T(8,128)(2,1)} %bitcast.1, f32[512,256]{1,0:T(8,128)} %gain_in.1, s32[23]{0:T(128)} %support_in.1, bf16[32,64]{1,0:T(8,128)(2,1)} %constant.14.clone.one_in, bf16[16,64,128]{2,1,0:T(8,128)(2,1)} %constant.15.clone.two_in, ...), custom_call_target="tpu_custom_call" | custom-call | tf_op jit(solution)/shard_map/pallas_call | solution.py:531
  72.4 1.8 %copy.13 = bf16[23,32,256]{2,1,0:T(8,128)(2,1)} copy(bf16[23,32,256]{2,1,0:T(8,128)(2,1)} %shard_map.109) | data formatting | bytes 753664
